TPU v7x, 256 devices: a whole 4x4x8 slice. The times are simulated.
256 devices in a mesh: grp: 16 (over z, core), seq: 16 (over x, y).
Axes of the slice: x: 4, y: 4, z: 8, core: 2. Of those that a mesh axis runs over, the one named last changes fastest.
Arguments:
- signal: bfloat16 [65536, 512], P(('grp', 'seq')), may hold values from -6 to 6
- gating: bfloat16 [65536, 512], P(('grp', 'seq')), may hold values from -6 to 6
- kernel: float32 [65536, 512], P(('grp', 'seq')), may hold values from -0.0234375 to 0.0234375
- bypass: float32 [512], replicated, may hold values from 0.5 to 1.5
Outputs:
- filtered: bfloat16 [65536, 512], P(('grp', 'seq'))
All inputs are finite; a program needn't handle non-finite values.
Results may differ from a plain program's by a relative error of at most 0.001.
Values sent between devices are 32-bit elements; how exact they have to be, the bound alone decides.
A program may use at most 64 MiB of HBM per device.

v0:
```python
import math

import jax
import jax.numpy as jnp
from jax import lax
from jax.sharding import PartitionSpec as P

HIGHEST = lax.Precision.HIGHEST


def phase_table(row_index, col_index, modulus):
    product = row_index[:, None] * col_index[None, :] % modulus
    angle = 2.0 * math.pi / modulus * product.astype(jnp.float32)
    return (jnp.cos(angle), jnp.sin(angle))


def split_length(length):
    factor = 1
    trial = 1
    while trial * trial <= length:
        if length % trial == 0:
            factor = trial
        trial += 1
    return factor


def transform(real_in, imag_in, direction):
    length = real_in.shape[0]
    trailing = real_in.shape[1:]
    first = split_length(length)
    second = length // first
    first_index = jnp.arange(first, dtype=jnp.int32)
    second_index = jnp.arange(second, dtype=jnp.int32)
    cos_first, sin_first = phase_table(first_index, first_index, first)
    sin_first = direction * sin_first
    source_real = real_in.reshape(first, second, -1)
    section_real = jnp.einsum("kn,nbm->kbm", cos_first, source_real, precision=HIGHEST)
    section_imag = jnp.einsum("kn,nbm->kbm", sin_first, source_real, precision=HIGHEST)
    if imag_in is not None:
        source_imag = imag_in.reshape(first, second, -1)
        section_real = section_real - jnp.einsum(
            "kn,nbm->kbm", sin_first, source_imag, precision=HIGHEST
        )
        section_imag = section_imag + jnp.einsum(
            "kn,nbm->kbm", cos_first, source_imag, precision=HIGHEST
        )
    cos_turn, sin_turn = phase_table(first_index, second_index, length)
    cos_turn = cos_turn[:, :, None]
    sin_turn = direction * sin_turn[:, :, None]
    turned_real = section_real * cos_turn - section_imag * sin_turn
    turned_imag = section_real * sin_turn + section_imag * cos_turn
    cos_second, sin_second = phase_table(second_index, second_index, second)
    sin_second = direction * sin_second
    final_real = jnp.einsum("kbm,bq->qkm", turned_real, cos_second, precision=HIGHEST) - jnp.einsum(
        "kbm,bq->qkm", turned_imag, sin_second, precision=HIGHEST
    )
    final_imag = jnp.einsum("kbm,bq->qkm", turned_real, sin_second, precision=HIGHEST) + jnp.einsum(
        "kbm,bq->qkm", turned_imag, cos_second, precision=HIGHEST
    )
    return (final_real.reshape((length,) + trailing), final_imag.reshape((length,) + trailing))


def spread_conv(signal_real, kernel):
    groups = lax.axis_size("grp")
    pieces = lax.axis_size("seq")
    devices = groups * pieces
    tok_rows, channels = signal_real.shape
    piece_rows = tok_rows // devices
    padded = 2 * devices * tok_rows
    position = lax.axis_index("grp") * pieces + lax.axis_index("seq")
    sent = (
        signal_real.reshape(groups, pieces, piece_rows, channels),
        kernel.reshape(groups, pieces, piece_rows, channels),
    )
    received = (
        lax.all_to_all(
            lax.all_to_all(sent[0], "grp", split_axis=0, concat_axis=0, tiled=True),
            "seq",
            split_axis=1,
            concat_axis=1,
            tiled=True,
        ),
        lax.all_to_all(
            lax.all_to_all(sent[1], "grp", split_axis=0, concat_axis=0, tiled=True),
            "seq",
            split_axis=1,
            concat_axis=1,
            tiled=True,
        ),
    )
    outer_index = jnp.arange(2 * devices, dtype=jnp.int32)
    local_pos = position * piece_rows + jnp.arange(piece_rows, dtype=jnp.int32)
    cos_twist, sin_twist = phase_table(outer_index, local_pos, padded)
    cos_twist = cos_twist[:, :, None]
    sin_twist = sin_twist[:, :, None]

    def outer_forward(pieces_in):
        flattened = pieces_in.reshape(devices, piece_rows * channels)
        extended = jnp.concatenate([flattened, jnp.zeros_like(flattened)], axis=0)
        real_part, imag_part = transform(extended, None, -1.0)
        real_part = real_part.reshape(2 * devices, piece_rows, channels)
        imag_part = imag_part.reshape(2 * devices, piece_rows, channels)
        twist_real = real_part * cos_twist + imag_part * sin_twist
        twist_imag = imag_part * cos_twist - real_part * sin_twist
        shape = (groups, pieces, 2, piece_rows, channels)
        return (twist_real.reshape(shape), twist_imag.reshape(shape))

    sig_real, sig_imag = outer_forward(received[0])
    ker_real, ker_imag = outer_forward(received[1])
    moved = (
        lax.all_to_all(
            lax.all_to_all(sig_real, "grp", split_axis=0, concat_axis=0, tiled=True),
            "seq",
            split_axis=1,
            concat_axis=1,
            tiled=True,
        ),
        lax.all_to_all(
            lax.all_to_all(sig_imag, "grp", split_axis=0, concat_axis=0, tiled=True),
            "seq",
            split_axis=1,
            concat_axis=1,
            tiled=True,
        ),
        lax.all_to_all(
            lax.all_to_all(ker_real, "grp", split_axis=0, concat_axis=0, tiled=True),
            "seq",
            split_axis=1,
            concat_axis=1,
            tiled=True,
        ),
        lax.all_to_all(
            lax.all_to_all(ker_imag, "grp", split_axis=0, concat_axis=0, tiled=True),
            "seq",
            split_axis=1,
            concat_axis=1,
            tiled=True,
        ),
    )
    inner_index = jnp.arange(tok_rows, dtype=jnp.int32)

    def to_rows(pieces_in):
        return jnp.transpose(pieces_in, (0, 1, 3, 2, 4)).reshape(tok_rows, 2, channels)

    def inner_forward(real_in, imag_in):
        real_part, imag_part = transform(to_rows(real_in), to_rows(imag_in), -1.0)
        return (jnp.transpose(real_part, (1, 0, 2)), jnp.transpose(imag_part, (1, 0, 2)))

    spec_real, spec_imag = inner_forward(moved[0], moved[1])
    kspec_real, kspec_imag = inner_forward(moved[2], moved[3])
    split_shape = (2, groups, pieces, piece_rows, channels)
    spread = (
        lax.all_to_all(
            lax.all_to_all(
                spec_real.reshape(split_shape), "grp", split_axis=1, concat_axis=1, tiled=True
            ),
            "seq",
            split_axis=2,
            concat_axis=2,
            tiled=True,
        ),
        lax.all_to_all(
            lax.all_to_all(
                spec_imag.reshape(split_shape), "grp", split_axis=1, concat_axis=1, tiled=True
            ),
            "seq",
            split_axis=2,
            concat_axis=2,
            tiled=True,
        ),
        lax.all_to_all(
            lax.all_to_all(
                kspec_real.reshape(split_shape), "grp", split_axis=1, concat_axis=1, tiled=True
            ),
            "seq",
            split_axis=2,
            concat_axis=2,
            tiled=True,
        ),
        lax.all_to_all(
            lax.all_to_all(
                kspec_imag.reshape(split_shape), "grp", split_axis=1, concat_axis=1, tiled=True
            ),
            "seq",
            split_axis=2,
            concat_axis=2,
            tiled=True,
        ),
    )
    natural = [
        jnp.transpose(part, (3, 1, 2, 0, 4)).reshape(2 * tok_rows, channels) for part in spread
    ]
    a_real = natural[0]
    a_imag = natural[1]
    b_real = natural[2]
    b_imag = natural[3]
    prod_real = a_real * b_real - a_imag * b_imag
    prod_imag = a_real * b_imag + a_imag * b_real
    back_shape = (piece_rows, groups, pieces, 2, channels)
    prod_real = jnp.transpose(prod_real.reshape(back_shape), (3, 1, 2, 0, 4))
    prod_imag = jnp.transpose(prod_imag.reshape(back_shape), (3, 1, 2, 0, 4))
    returned = (
        lax.all_to_all(
            lax.all_to_all(prod_real, "grp", split_axis=1, concat_axis=1, tiled=True),
            "seq",
            split_axis=2,
            concat_axis=2,
            tiled=True,
        ),
        lax.all_to_all(
            lax.all_to_all(prod_imag, "grp", split_axis=1, concat_axis=1, tiled=True),
            "seq",
            split_axis=2,
            concat_axis=2,
            tiled=True,
        ),
    )
    prod_real = returned[0].reshape(2, tok_rows, channels)
    prod_imag = returned[1].reshape(2, tok_rows, channels)
    back_real, back_imag = transform(
        jnp.transpose(prod_real, (1, 0, 2)), jnp.transpose(prod_imag, (1, 0, 2)), 1.0
    )
    back_real = jnp.transpose(back_real, (1, 0, 2))
    back_imag = jnp.transpose(back_imag, (1, 0, 2))
    own_outer = 2 * position + jnp.arange(2, dtype=jnp.int32)
    cos_back, sin_back = phase_table(own_outer, inner_index, padded)
    cos_back = cos_back[:, :, None]
    sin_back = sin_back[:, :, None]
    twist_real = (back_real * cos_back - back_imag * sin_back).reshape(split_shape)
    twist_imag = (back_real * sin_back + back_imag * cos_back).reshape(split_shape)
    gathered = (
        lax.all_to_all(
            lax.all_to_all(twist_real, "grp", split_axis=1, concat_axis=1, tiled=True),
            "seq",
            split_axis=2,
            concat_axis=2,
            tiled=True,
        ),
        lax.all_to_all(
            lax.all_to_all(twist_imag, "grp", split_axis=1, concat_axis=1, tiled=True),
            "seq",
            split_axis=2,
            concat_axis=2,
            tiled=True,
        ),
    )

    def to_outer(pieces_in):
        return jnp.transpose(pieces_in, (1, 2, 0, 3, 4)).reshape(2 * devices, piece_rows * channels)

    final_real, final_imag = transform(to_outer(gathered[0]), to_outer(gathered[1]), 1.0)
    values = (final_real[:devices] * (1.0 / padded)).reshape(groups, pieces, piece_rows, channels)
    conv = lax.all_to_all(
        lax.all_to_all(values, "grp", split_axis=0, concat_axis=0, tiled=True),
        "seq",
        split_axis=1,
        concat_axis=1,
        tiled=True,
    )
    return conv.reshape(tok_rows, channels)


def on_device(signal, gating, kernel, bypass):
    signal_real = signal.astype(jnp.float32)
    conv = spread_conv(signal_real, kernel)
    mixed = (conv + bypass[None, :] * signal_real) * gating.astype(jnp.float32)
    return mixed.astype(jnp.bfloat16)


def solution(mesh):
    placed = (P(("grp", "seq"), None), P(("grp", "seq"), None), P(("grp", "seq"), None), P())
    return jax.shard_map(
        on_device, mesh=mesh, in_specs=placed, out_specs=P(("grp", "seq"), None), check_vma=False
    )
```

profile of v0, /device:TPU:1, one launch (start us, length us, event | category | flops | bytes accessed | tf_op | source)
XLA Modules:
  0.0 843.9 jit_solution(2757082908982444671)
XLA Ops:
  1.0 27.1 %all_to_all.150 = f32[16,16,1,512]{3,1,2,0:T(8,128)S(1)} all-to-all(f32[16,16,1,512]{3,1,2,0:T(8,128)S(1)} %convert), channel_id=1, replica_groups=mesh['grp'=16,'seq'=16] {'grp'}, dimensions={0} | all-to-all | bytes 1048576 | tf_op jit(solution)/shard_map/all_to_all | solution.py:77
  32.7 15.6 %all-to-all-done.8 = f32[16,16,1,512]{3,1,2,0:T(8,128)S(1)} async-done(((f32[16,16,1,512]{3,1,2,0:T(8,128)}), f32[16,16,1,512]{3,1,2,0:T(8,128)S(1)}, u32[]{:S(2)}, u32[]{:S(2)}) %all-to-all-start.8) | async-done | bytes 524320 | tf_op jit(solution)/shard_map/all_to_all | solution.py:84
  48.3 6.8 all-to-all-start.1
  56.7 9.8 %all-to-all-done.1 = f32[16,16,1,512]{3,0,2,1:T(8,128)S(1)} async-done(((f32[16,16,1,512]{3,0,2,1:T(8,128)}), f32[16,16,1,512]{3,0,2,1:T(8,128)S(1)}, u32[]{:S(2)}, u32[]{:S(2)}) %all-to-all-start.1) | async-done | bytes 524320 | tf_op jit(solution)/shard_map/all_to_all | solution.py:76
  73.6 6.8 all-to-all-done.9
  122.1 33.1 %all_to_all.151 = f32[16,16,2,1,512]{4,2,1,3,0:T(2,128)S(1)} all-to-all(f32[16,16,2,1,512]{4,2,1,3,0:T(2,128)S(1)} %get-tuple-element.9), channel_id=1, replica_groups=mesh['grp'=16,'seq'=16] {'grp'}, dimensions={0} | all-to-all | bytes 2097152 | tf_op jit(solution)/shard_map/all_to_all | solution.py:133
  155.2 31.3 %all_to_all.152 = f32[16,16,2,1,512]{4,2,1,3,0:T(2,128)S(1)} all-to-all(f32[16,16,2,1,512]{4,2,1,3,0:T(2,128)S(1)} %get-tuple-element.10), channel_id=1, replica_groups=mesh['grp'=16,'seq'=16] {'grp'}, dimensions={0} | all-to-all | bytes 2097152 | tf_op jit(solution)/shard_map/all_to_all | solution.py:126
  186.4 31.3 %all_to_all.153 = f32[16,16,2,1,512]{4,2,1,3,0:T(2,128)} all-to-all(f32[16,16,2,1,512]{4,2,1,3,0:T(2,128)S(1)} %get-tuple-element.25), channel_id=1, replica_groups=mesh['grp'=16,'seq'=16] {'grp'}, dimensions={0} | all-to-all | bytes 2097152 | tf_op jit(solution)/shard_map/all_to_all | solution.py:112
  222.8 25.8 %all-to-all-done.4 = f32[16,16,2,1,512]{4,2,1,3,0:T(2,128)S(1)} async-done(((f32[16,16,2,1,512]{4,2,1,3,0:T(2,128)}), f32[16,16,2,1,512]{4,2,1,3,0:T(2,128)S(1)}, u32[]{:S(2)}, u32[]{:S(2)}) %all-to-all-start.4) | async-done | bytes 1048608 | tf_op jit(solution)/shard_map/all_to_all | solution.py:119
  255.1 14.5 %all-to-all-done.11 = f32[16,16,2,1,512]{4,2,0,3,1:T(2,128)S(1)} async-done(((f32[16,16,2,1,512]{4,2,0,3,1:T(2,128)}), f32[16,16,2,1,512]{4,2,0,3,1:T(2,128)S(1)}, u32[]{:S(2)}, u32[]{:S(2)}) %all-to-all-start.11) | async-done | bytes 1048608 | tf_op jit(solution)/shard_map/all_to_all | solution.py:125
  275.4 17.0 %all-to-all-done.3 = f32[16,16,2,1,512]{4,2,0,3,1:T(2,128)} async-done(((f32[16,16,2,1,512]{4,2,0,3,1:T(2,128)}), f32[16,16,2,1,512]{4,2,0,3,1:T(2,128)}, u32[]{:S(2)}, u32[]{:S(2)}) %all-to-all-start.3) | async-done | bytes 1048608 | tf_op jit(solution)/shard_map/all_to_all | solution.py:111
  304.8 7.7 all-to-all-done.5
  343.6 8.1 all-to-all-start.14
  357.3 22.5 %all-to-all-done.14 = f32[2,16,16,1,512]{4,0,2,3,1:T(2,128)} async-done(((f32[2,16,16,1,512]{4,0,2,3,1:T(2,128)}), f32[2,16,16,1,512]{4,0,2,3,1:T(2,128)}, u32[]{:S(2)}, u32[]{:S(2)}) %all-to-all-start.14) | async-done | bytes 1048608 | tf_op jit(solution)/shard_map/all_to_all | solution.py:172
  391.3 20.1 %all-to-all-done.18 = f32[2,16,16,1,512]{4,0,2,3,1:T(2,128)S(1)} async-done(((f32[2,16,16,1,512]{4,0,2,3,1:T(2,128)}), f32[2,16,16,1,512]{4,0,2,3,1:T(2,128)S(1)}, u32[]{:S(2)}, u32[]{:S(2)}) %all-to-all-start.18) | async-done | bytes 1048608 | tf_op jit(solution)/shard_map/all_to_all | solution.py:181
  421.4 20.7 %all-to-all-done.6 = f32[2,16,16,1,512]{4,0,2,3,1:T(2,128)} async-done(((f32[2,16,16,1,512]{4,0,2,3,1:T(2,128)}), f32[2,16,16,1,512]{4,0,2,3,1:T(2,128)}, u32[]{:S(2)}, u32[]{:S(2)}) %all-to-all-start.6) | async-done | bytes 1048608 | tf_op jit(solution)/shard_map/all_to_all | solution.py:154
  449.2 25.2 %all-to-all-done.16 = f32[2,16,16,1,512]{4,0,2,3,1:T(2,128)S(1)} async-done(((f32[2,16,16,1,512]{4,0,2,3,1:T(2,128)}), f32[2,16,16,1,512]{4,0,2,3,1:T(2,128)S(1)}, u32[]{:S(2)}, u32[]{:S(2)}) %all-to-all-start.16) | async-done | bytes 1048608 | tf_op jit(solution)/shard_map/all_to_all | solution.py:163
  479.6 15.8 %all-to-all-done.15 = f32[2,16,16,1,512]{4,0,1,3,2:T(2,128)S(1)} async-done(((f32[2,16,16,1,512]{4,0,1,3,2:T(2,128)}), f32[2,16,16,1,512]{4,0,1,3,2:T(2,128)S(1)}, u32[]{:S(2)}, u32[]{:S(2)}) %all-to-all-start.15) | async-done | bytes 1048608 | tf_op jit(solution)/shard_map/all_to_all | solution.py:171
  502.8 15.3 %all-to-all-done.19 = f32[2,16,16,1,512]{4,0,1,3,2:T(2,128)S(1)} async-done(((f32[2,16,16,1,512]{4,0,1,3,2:T(2,128)}), f32[2,16,16,1,512]{4,0,1,3,2:T(2,128)S(1)}, u32[]{:S(2)}, u32[]{:S(2)}) %all-to-all-start.19) | async-done | bytes 1048608 | tf_op jit(solution)/shard_map/all_to_all | solution.py:180
  522.9 15.0 %all-to-all-done.7 = f32[2,16,16,1,512]{4,0,1,3,2:T(2,128)} async-done(((f32[2,16,16,1,512]{4,0,1,3,2:T(2,128)}), f32[2,16,16,1,512]{4,0,1,3,2:T(2,128)}, u32[]{:S(2)}, u32[]{:S(2)}) %all-to-all-start.7) | async-done | bytes 1048608 | tf_op jit(solution)/shard_map/all_to_all | solution.py:153
  537.9 18.4 %all_to_all.154 = f32[2,16,16,1,512]{4,0,1,3,2:T(2,128)S(1)} all-to-all(f32[2,16,16,1,512]{4,0,1,3,2:T(2,128)S(1)} %copy.341), channel_id=1, replica_groups=mesh['grp'=16,'seq'=16] {'seq'}, dimensions={2} | all-to-all | bytes 2097152 | tf_op jit(solution)/shard_map/all_to_all | solution.py:162
  559.7 6.8 all-to-all-start.20
  568.0 26.4 %all-to-all-done.20 = f32[2,16,16,1,512]{4,0,2,3,1:T(2,128)S(1)} async-done(((f32[2,16,16,1,512]{4,0,2,3,1:T(2,128)}), f32[2,16,16,1,512]{4,0,2,3,1:T(2,128)S(1)}, u32[]{:S(2)}, u32[]{:S(2)}) %all-to-all-start.20) | async-done | bytes 1048608 | tf_op jit(solution)/shard_map/all_to_all | solution.py:204
  599.6 26.3 %all-to-all-done.22 = f32[2,16,16,1,512]{4,0,2,3,1:T(2,128)S(1)} async-done(((f32[2,16,16,1,512]{4,0,2,3,1:T(2,128)}), f32[2,16,16,1,512]{4,0,2,3,1:T(2,128)S(1)}, u32[]{:S(2)}, u32[]{:S(2)}) %all-to-all-start.22) | async-done | bytes 1048608 | tf_op jit(solution)/shard_map/all_to_all | solution.py:211
  631.1 15.8 %all-to-all-done.21 = f32[2,16,16,1,512]{4,0,1,3,2:T(2,128)S(1)} async-done(((f32[2,16,16,1,512]{4,0,1,3,2:T(2,128)}), f32[2,16,16,1,512]{4,0,1,3,2:T(2,128)S(1)}, u32[]{:S(2)}, u32[]{:S(2)}) %all-to-all-start.21) | async-done | bytes 1048608 | tf_op jit(solution)/shard_map/all_to_all | solution.py:203
  657.4 12.2 %all-to-all-done.23 = f32[2,16,16,1,512]{4,0,1,3,2:T(2,128)} async-done(((f32[2,16,16,1,512]{4,0,1,3,2:T(2,128)}), f32[2,16,16,1,512]{4,0,1,3,2:T(2,128)}, u32[]{:S(2)}, u32[]{:S(2)}) %all-to-all-start.23) | async-done | bytes 1048608 | tf_op jit(solution)/shard_map/all_to_all | solution.py:210
  698.4 26.8 %all-to-all-done.24 = f32[2,16,16,1,512]{4,2,0,3,1:T(8,128)S(1)} async-done(((f32[2,16,16,1,512]{4,2,0,3,1:T(8,128)}), f32[2,16,16,1,512]{4,2,0,3,1:T(8,128)S(1)}, u32[]{:S(2)}, u32[]{:S(2)}) %all-to-all-start.24) | async-done | bytes 1048608 | tf_op jit(solution)/shard_map/all_to_all | solution.py:233
  730.4 26.3 %all-to-all-done.26 = f32[2,16,16,1,512]{4,2,0,3,1:T(8,128)S(1)} async-done(((f32[2,16,16,1,512]{4,2,0,3,1:T(8,128)}), f32[2,16,16,1,512]{4,2,0,3,1:T(8,128)S(1)}, u32[]{:S(2)}, u32[]{:S(2)}) %all-to-all-start.26) | async-done | bytes 1048608 | tf_op jit(solution)/shard_map/all_to_all | solution.py:240
  761.9 15.7 %all-to-all-done.25 = f32[2,16,16,1,512]{4,1,0,3,2:T(8,128)S(1)} async-done(((f32[2,16,16,1,512]{4,1,0,3,2:T(8,128)}), f32[2,16,16,1,512]{4,1,0,3,2:T(8,128)S(1)}, u32[]{:S(2)}, u32[]{:S(2)}) %all-to-all-start.25) | async-done | bytes 1048608 | tf_op jit(solution)/shard_map/all_to_all | solution.py:232
  784.6 14.8 %all-to-all-done.27 = f32[2,16,16,1,512]{4,1,0,3,2:T(8,128)S(1)} async-done(((f32[2,16,16,1,512]{4,1,0,3,2:T(8,128)}), f32[2,16,16,1,512]{4,1,0,3,2:T(8,128)S(1)}, u32[]{:S(2)}, u32[]{:S(2)}) %all-to-all-start.27) | async-done | bytes 1048608 | tf_op jit(solution)/shard_map/all_to_all | solution.py:239
  806.6 20.8 %all_to_all.155 = f32[16,16,1,512]{3,1,2,0:T(8,128)S(1)} all-to-all(f32[16,16,1,512]{3,1,2,0:T(8,128)S(1)} %copy.382), channel_id=1, replica_groups=mesh['grp'=16,'seq'=16] {'grp'}, dimensions={0} | all-to-all | bytes 1048576 | tf_op jit(solution)/shard_map/all_to_all | solution.py:254
  827.7 14.2 %all_to_all.156 = f32[16,16,1,512]{3,0,2,1:T(8,128)S(1)} all-to-all(f32[16,16,1,512]{3,0,2,1:T(8,128)S(1)} %copy.383), channel_id=1, replica_groups=mesh['grp'=16,'seq'=16] {'seq'}, dimensions={1} | all-to-all | bytes 1048576 | tf_op jit(solution)/shard_map/all_to_all | solution.py:253
  (167 shorter events, 249.3 us)
Async XLA Ops:
  28.1 20.2 %all-to-all-start.8 = ((f32[16,16,1,512]{3,1,2,0:T(8,128)}), f32[16,16,1,512]{3,1,2,0:T(8,128)S(1)}, u32[]{:S(2)}, u32[]{:S(2)}) async-start(f32[16,16,1,512]{3,1,2,0:T(8,128)} %bitcast.17), calls=%async_computation.8 | async-start | bytes 1048576 | tf_op jit(solution)/shard_map/all_to_all | solution.py:84
  48.3 18.3 %all-to-all-start.1 = ((f32[16,16,1,512]{3,0,2,1:T(8,128)}), f32[16,16,1,512]{3,0,2,1:T(8,128)S(1)}, u32[]{:S(2)}, u32[]{:S(2)}) async-start(f32[16,16,1,512]{3,0,2,1:T(8,128)} %copy.289), calls=%async_computation.1 | async-start | bytes 1048576 | tf_op jit(solution)/shard_map/all_to_all | solution.py:76
  66.5 13.9 %all-to-all-start.9 = ((f32[16,16,1,512]{3,0,2,1:T(8,128)}), f32[16,16,1,512]{3,0,2,1:T(8,128)S(1)}, u32[]{:S(2)}, u32[]{:S(2)}) async-start(f32[16,16,1,512]{3,0,2,1:T(8,128)} %copy.314), calls=%async_computation.9 | async-start | bytes 1048576 | tf_op jit(solution)/shard_map/all_to_all | solution.py:83
  103.3 3.9 copy-start.6
  217.7 30.9 %all-to-all-start.4 = ((f32[16,16,2,1,512]{4,2,1,3,0:T(2,128)}), f32[16,16,2,1,512]{4,2,1,3,0:T(2,128)S(1)}, u32[]{:S(2)}, u32[]{:S(2)}) async-start(f32[16,16,2,1,512]{4,2,1,3,0:T(2,128)} %get-tuple-element.26), calls=%async_computation.4 | async-start | bytes 2097152 | tf_op jit(solution)/shard_map/all_to_all | solution.py:119
  248.6 21.0 %all-to-all-start.11 = ((f32[16,16,2,1,512]{4,2,0,3,1:T(2,128)}), f32[16,16,2,1,512]{4,2,0,3,1:T(2,128)S(1)}, u32[]{:S(2)}, u32[]{:S(2)}) async-start(f32[16,16,2,1,512]{4,2,0,3,1:T(2,128)} %copy.325), calls=%async_computation.11 | async-start | bytes 2097152 | tf_op jit(solution)/shard_map/all_to_all | solution.py:125
  269.6 22.9 %all-to-all-start.3 = ((f32[16,16,2,1,512]{4,2,0,3,1:T(2,128)}), f32[16,16,2,1,512]{4,2,0,3,1:T(2,128)}, u32[]{:S(2)}, u32[]{:S(2)}) async-start(f32[16,16,2,1,512]{4,2,0,3,1:T(2,128)} %copy.302), calls=%async_computation.3 | async-start | bytes 2097152 | tf_op jit(solution)/shard_map/all_to_all | solution.py:111
  292.4 20.0 %all-to-all-start.5 = ((f32[16,16,2,1,512]{4,2,0,3,1:T(2,128)}), f32[16,16,2,1,512]{4,2,0,3,1:T(2,128)}, u32[]{:S(2)}, u32[]{:S(2)}) async-start(f32[16,16,2,1,512]{4,2,0,3,1:T(2,128)} %copy.304), calls=%async_computation.5 | async-start | bytes 2097152 | tf_op jit(solution)/shard_map/all_to_all | solution.py:118
  312.4 18.6 %all-to-all-start.13 = ((f32[16,16,2,1,512]{4,2,0,3,1:T(2,128)}), f32[16,16,2,1,512]{4,2,0,3,1:T(2,128)}, u32[]{:S(2)}, u32[]{:S(2)}) async-start(f32[16,16,2,1,512]{4,2,0,3,1:T(2,128)} %copy.327), calls=%async_computation.13 | async-start | bytes 2097152 | tf_op jit(solution)/shard_map/all_to_all | solution.py:132
  321.2 2.0 copy-start.7
  327.3 5.9 copy-start.8
  333.2 1.5 copy-start.4
  333.2 1.8 copy-start.5
  337.5 1.6 copy-start.1
  343.6 8.1 copy-start.2
  343.6 36.2 %all-to-all-start.14 = ((f32[2,16,16,1,512]{4,0,2,3,1:T(2,128)}), f32[2,16,16,1,512]{4,0,2,3,1:T(2,128)}, u32[]{:S(2)}, u32[]{:S(2)}) async-start(f32[2,16,16,1,512]{4,0,2,3,1:T(2,128)} %bitcast.221), calls=%async_computation.14 | async-start | bytes 2097152 | tf_op jit(solution)/shard_map/all_to_all | solution.py:172
  379.8 3.7 copy-start
  379.8 31.6 %all-to-all-start.18 = ((f32[2,16,16,1,512]{4,0,2,3,1:T(2,128)}), f32[2,16,16,1,512]{4,0,2,3,1:T(2,128)S(1)}, u32[]{:S(2)}, u32[]{:S(2)}) async-start(f32[2,16,16,1,512]{4,0,2,3,1:T(2,128)} %bitcast.220), calls=%async_computation.18 | async-start | bytes 2097152 | tf_op jit(solution)/shard_map/all_to_all | solution.py:181
  411.4 30.7 %all-to-all-start.6 = ((f32[2,16,16,1,512]{4,0,2,3,1:T(2,128)}), f32[2,16,16,1,512]{4,0,2,3,1:T(2,128)}, u32[]{:S(2)}, u32[]{:S(2)}) async-start(f32[2,16,16,1,512]{4,0,2,3,1:T(2,128)} %bitcast.219), calls=%async_computation.6 | async-start | bytes 2097152 | tf_op jit(solution)/shard_map/all_to_all | solution.py:154
  442.0 32.4 %all-to-all-start.16 = ((f32[2,16,16,1,512]{4,0,2,3,1:T(2,128)}), f32[2,16,16,1,512]{4,0,2,3,1:T(2,128)S(1)}, u32[]{:S(2)}, u32[]{:S(2)}) async-start(f32[2,16,16,1,512]{4,0,2,3,1:T(2,128)} %bitcast.30), calls=%async_computation.16 | async-start | bytes 2097152 | tf_op jit(solution)/shard_map/all_to_all | solution.py:163
  474.4 21.0 %all-to-all-start.15 = ((f32[2,16,16,1,512]{4,0,1,3,2:T(2,128)}), f32[2,16,16,1,512]{4,0,1,3,2:T(2,128)S(1)}, u32[]{:S(2)}, u32[]{:S(2)}) async-start(f32[2,16,16,1,512]{4,0,1,3,2:T(2,128)} %copy.334), calls=%async_computation.15 | async-start | bytes 2097152 | tf_op jit(solution)/shard_map/all_to_all | solution.py:171
  496.4 21.7 %all-to-all-start.19 = ((f32[2,16,16,1,512]{4,0,1,3,2:T(2,128)}), f32[2,16,16,1,512]{4,0,1,3,2:T(2,128)S(1)}, u32[]{:S(2)}, u32[]{:S(2)}) async-start(f32[2,16,16,1,512]{4,0,1,3,2:T(2,128)} %copy.348), calls=%async_computation.19 | async-start | bytes 2097152 | tf_op jit(solution)/shard_map/all_to_all | solution.py:180
  518.0 19.9 %all-to-all-start.7 = ((f32[2,16,16,1,512]{4,0,1,3,2:T(2,128)}), f32[2,16,16,1,512]{4,0,1,3,2:T(2,128)}, u32[]{:S(2)}, u32[]{:S(2)}) async-start(f32[2,16,16,1,512]{4,0,1,3,2:T(2,128)} %copy.313), calls=%async_computation.7 | async-start | bytes 2097152 | tf_op jit(solution)/shard_map/all_to_all | solution.py:153
  522.9 33.4 %copy-start.10 = (f32[2,16,16,1,512]{4,0,1,3,2:T(2,128)S(1)}, f32[2,16,16,1,512]{4,0,1,3,2:T(2,128)}, u32[]{:S(2)}) copy-start(f32[2,16,16,1,512]{4,0,1,3,2:T(2,128)} %copy-done.9) | copy-start | bytes 3145732
  559.7 34.8 %all-to-all-start.20 = ((f32[2,16,16,1,512]{4,0,2,3,1:T(2,128)}), f32[2,16,16,1,512]{4,0,2,3,1:T(2,128)S(1)}, u32[]{:S(2)}, u32[]{:S(2)}) async-start(f32[2,16,16,1,512]{4,0,2,3,1:T(2,128)} %copy.349), calls=%async_computation.20 | async-start | bytes 2097152 | tf_op jit(solution)/shard_map/all_to_all | solution.py:204
  594.4 31.5 %all-to-all-start.22 = ((f32[2,16,16,1,512]{4,0,2,3,1:T(2,128)}), f32[2,16,16,1,512]{4,0,2,3,1:T(2,128)S(1)}, u32[]{:S(2)}, u32[]{:S(2)}) async-start(f32[2,16,16,1,512]{4,0,2,3,1:T(2,128)} %copy.354), calls=%async_computation.22 | async-start | bytes 2097152 | tf_op jit(solution)/shard_map/all_to_all | solution.py:211
  625.9 21.0 %all-to-all-start.21 = ((f32[2,16,16,1,512]{4,0,1,3,2:T(2,128)}), f32[2,16,16,1,512]{4,0,1,3,2:T(2,128)S(1)}, u32[]{:S(2)}, u32[]{:S(2)}) async-start(f32[2,16,16,1,512]{4,0,1,3,2:T(2,128)} %copy.350), calls=%async_computation.21 | async-start | bytes 2097152 | tf_op jit(solution)/shard_map/all_to_all | solution.py:203
  646.8 22.7 %all-to-all-start.23 = ((f32[2,16,16,1,512]{4,0,1,3,2:T(2,128)}), f32[2,16,16,1,512]{4,0,1,3,2:T(2,128)}, u32[]{:S(2)}, u32[]{:S(2)}) async-start(f32[2,16,16,1,512]{4,0,1,3,2:T(2,128)} %copy.355), calls=%async_computation.23 | async-start | bytes 2097152 | tf_op jit(solution)/shard_map/all_to_all | solution.py:210
  692.8 32.3 %all-to-all-start.24 = ((f32[2,16,16,1,512]{4,2,0,3,1:T(8,128)}), f32[2,16,16,1,512]{4,2,0,3,1:T(8,128)S(1)}, u32[]{:S(2)}, u32[]{:S(2)}) async-start(f32[2,16,16,1,512]{4,2,0,3,1:T(8,128)} %copy.375), calls=%async_computation.24 | async-start | bytes 2097152 | tf_op jit(solution)/shard_map/all_to_all | solution.py:233
  725.2 31.5 %all-to-all-start.26 = ((f32[2,16,16,1,512]{4,2,0,3,1:T(8,128)}), f32[2,16,16,1,512]{4,2,0,3,1:T(8,128)S(1)}, u32[]{:S(2)}, u32[]{:S(2)}) async-start(f32[2,16,16,1,512]{4,2,0,3,1:T(8,128)} %copy.378), calls=%async_computation.26 | async-start | bytes 2097152 | tf_op jit(solution)/shard_map/all_to_all | solution.py:240
  756.6 21.0 %all-to-all-start.25 = ((f32[2,16,16,1,512]{4,1,0,3,2:T(8,128)}), f32[2,16,16,1,512]{4,1,0,3,2:T(8,128)S(1)}, u32[]{:S(2)}, u32[]{:S(2)}) async-start(f32[2,16,16,1,512]{4,1,0,3,2:T(8,128)} %copy.376), calls=%async_computation.25 | async-start | bytes 2097152 | tf_op jit(solution)/shard_map/all_to_all | solution.py:232
  777.6 21.8 %all-to-all-start.27 = ((f32[2,16,16,1,512]{4,1,0,3,2:T(8,128)}), f32[2,16,16,1,512]{4,1,0,3,2:T(8,128)S(1)}, u32[]{:S(2)}, u32[]{:S(2)}) async-start(f32[2,16,16,1,512]{4,1,0,3,2:T(8,128)} %copy.379), calls=%async_computation.27 | async-start | bytes 2097152 | tf_op jit(solution)/shard_map/all_to_all | solution.py:239
  (5 other events, 5.3 us)
where the time goes:
time: 857 us; the launch traced here: 844 us
  waiting for transfers between devices  400 us (47%)
  blocking collectives  176 us (21%)
  starting transfers between devices  100 us (12%)
  local copies, waits for them, and re-layouts  83.1 us (10%)
  matrix products  74.5 us (9%)
  other arithmetic  9.19 us (1%)
    all_to_all x1, blocking collectives, spread_conv(): lax.all_to_all(ker_imag, 'grp', split_axis=0, concat_axis=0, tiled=True)  33.1 us
    all_to_all x1, blocking collectives, spread_conv(): lax.all_to_all(sig_real, 'grp', split_axis=0, concat_axis=0, tiled=True)  31.3 us
    all_to_all x1, blocking collectives, spread_conv(): lax.all_to_all(ker_real, 'grp', split_axis=0, concat_axis=0, tiled=True)  31.3 us
    all_to_all x1, blocking collectives, spread_conv(): lax.all_to_all(sent[0], 'grp', split_axis=0, concat_axis=0, tiled=True)  27.1 us
    all_to_all x1, waiting for transfers between devices, spread_conv(): lax.all_to_all(twist_real, 'grp', split_axis=1, concat_axis=1, tiled=True)  26.8 us
    all_to_all x1, waiting for transfers between devices, spread_conv(): lax.all_to_all(prod_real, 'grp', split_axis=1, concat_axis=1, tiled=True)  26.4 us
    all_to_all x1, waiting for transfers between devices, spread_conv(): lax.all_to_all(prod_imag, 'grp', split_axis=1, concat_axis=1, tiled=True)  26.3 us
    all_to_all x1, waiting for transfers between devices, spread_conv(): lax.all_to_all(twist_imag, 'grp', split_axis=1, concat_axis=1, tiled=True)  26.3 us
  transfers between devices with their start and end apart: 23, of which 23 were waited for; matrix products, arithmetic and copies ran while one was open for 9% of the time, Pallas kernels for 0%

commit v1 on v0

v1 whole, which is shorter than its diff:
```python
import functools

import jax
import jax.numpy as jnp
import ml_dtypes
import numpy as np
from jax import lax
from jax.experimental import pallas as pl
from jax.experimental.pallas import tpu as pltpu
from jax.sharding import PartitionSpec as P

MESH = pl.DeviceIdType.MESH
F32 = jnp.float32
BF16 = jnp.bfloat16
ROWS = 256
CHIPS = 128
TOKENS = 65536


def split_table(table):
    high = table.astype(ml_dtypes.bfloat16)
    low = (table - high.astype(np.float64)).astype(ml_dtypes.bfloat16)
    return high, low


def tables():
    row = np.arange(256)
    core, chip = row // CHIPS, row % CHIPS
    n1 = 32 * (chip // 16) + 16 * core + chip % 16
    index = np.arange(256)
    quarter = 4 * index - 1

    first = 2.0 * np.pi / 1024 * (quarter[:, None] * n1[None, :] % 1024)
    first_high, first_low = split_table(np.concatenate([np.cos(first), -np.sin(first)], axis=0))
    first_all = np.concatenate([first_high, first_low, first_high], axis=1)

    turn = 2.0 * np.pi / (4 * TOKENS) * (quarter[:, None] * index[None, :] % (4 * TOKENS))
    turn_all = np.concatenate([np.cos(turn), -np.sin(turn)], axis=1).astype(np.float32)

    second = 2.0 * np.pi / 256 * (index[:, None] * index[None, :] % 256)
    cos, sin = np.cos(second), np.sin(second)
    forward = np.concatenate(split_table(np.block([[cos, -sin], [sin, cos]])), axis=0)
    backward = np.concatenate(split_table(np.block([[cos, sin], [-sin, cos]])), axis=0)

    last = np.concatenate([np.cos(first.T), -np.sin(first.T)], axis=1) / TOKENS
    last_high, last_low = split_table(last)
    last_all = np.concatenate([last_high, last_low, last_high], axis=1)
    return first_all, turn_all, forward, backward, last_all


def dot(a, b):
    return jnp.dot(a, b, preferred_element_type=F32)


def halves(x):
    high = x.astype(BF16)
    return high, (x - high.astype(F32)).astype(BF16)


def kernel_body(
    sig_hbm, gate_hbm, ker_hbm, byp_ref, first_hbm, turn_hbm, fwd_hbm, bwd_hbm, last_hbm,
    out_ref,
    sig, gate, ker, first, turn, fwd, bwd, last,
    wide, sib_u, sib_k, send, recv, a_buf, b_buf, x_buf, p_buf, c_buf, d_buf, y_buf, y_sib, y_send, y_recv,
    load_sem, sib_send, sib_recv, send_sem, recv_sem, round_sem,
):
    grp, seq = lax.axis_index("grp"), lax.axis_index("seq")
    z, core = grp // 2, grp % 2
    other = 1 - core
    chip = z * 16 + seq
    sibling = (z * 2 + other, seq)

    barrier = pltpu.get_barrier_semaphore()
    pl.semaphore_signal(barrier, inc=1, device_id=sibling, device_id_type=MESH)
    for j in range(1, 8):
        pl.semaphore_signal(barrier, inc=1, device_id=((z + j) % 8 * 2 + core, seq), device_id_type=MESH)
    for j in range(1, 16):
        pl.semaphore_signal(barrier, inc=1, device_id=(grp, (seq + j) % 16), device_id_type=MESH)

    loads = [
        pltpu.make_async_copy(source, target, load_sem.at[i])
        for i, (source, target) in enumerate(
            [
                (ker_hbm, ker), (sig_hbm, sig), (first_hbm, first), (turn_hbm, turn),
                (fwd_hbm, fwd), (bwd_hbm, bwd), (last_hbm, last), (gate_hbm, gate),
            ]
        )
    ]
    for load in loads:
        load.start()
    loads[0].wait()
    loads[1].wait()
    wide[...] = sig[...].astype(F32)

    pl.semaphore_wait(barrier, 23)
    far_lanes = pl.ds(pl.multiple_of(other * 256, 256), 256)
    near_lanes = pl.multiple_of(core * 256, 256)
    swaps = [
        pltpu.make_async_remote_copy(
            src_ref=source.at[:, far_lanes], dst_ref=target, send_sem=sib_send.at[i], recv_sem=sib_recv.at[i],
            device_id=sibling, device_id_type=MESH,
        )
        for i, (source, target) in enumerate([(ker, sib_k), (wide, sib_u)])
    ]
    for swap in swaps:
        swap.start()
    for j in range(1, 8):
        pl.semaphore_signal(round_sem, inc=1, device_id=((z + j) % 8 * 2 + core, seq), device_id_type=MESH)

    def place(block, ab, start):
        send[pl.ds(ab * 1024 + start, CHIPS, stride=8), :] = block.T

    for ab in range(2):
        for half in range(2):
            rows = pl.ds(half * 128, 128)
            lanes = pl.ds(near_lanes + ab * 128, 128)
            place(wide[rows, lanes], ab, 2 * core + half)
            place(ker[rows, lanes], ab, 4 + 2 * core + half)
    swaps[0].wait_recv()
    swaps[1].wait_recv()
    for ab in range(2):
        for half in range(2):
            rows, lanes = pl.ds(half * 128, 128), pl.ds(ab * 128, 128)
            place(sib_u[rows, lanes], ab, 2 * other + half)
            place(sib_k[rows, lanes], ab, 4 + 2 * other + half)
    pl.semaphore_wait(round_sem, 7)

    def spread(source, target, base, sends, receives):
        def step(i, carry):
            to_z, to_x, to_y = (z + i % 8) % 8, (seq // 4 + i // 8 % 4) % 4, (seq % 4 + i // 32) % 4
            to_seq = to_x * 4 + to_y
            to_chip = to_z * 16 + to_seq
            pltpu.make_async_remote_copy(
                src_ref=source.at[pl.ds(pl.multiple_of(base + to_chip * 8, 8), 8)],
                dst_ref=target.at[pl.ds(pl.multiple_of(base + chip * 8, 8), 8)],
                send_sem=sends, recv_sem=receives,
                device_id=(to_z * 2 + core, to_seq), device_id_type=MESH,
            ).start()
            return carry

        lax.fori_loop(1, CHIPS, step, 0)
        own = pl.ds(pl.multiple_of(base + chip * 8, 8), 8)
        target[own, :] = source[own, :]

    def drain(buffer, semaphore):
        slabs = buffer.at[pl.ds(0, (CHIPS - 1) * 8)]
        pltpu.make_async_copy(slabs, slabs, semaphore).wait()

    for ab in range(2):
        spread(send, recv, ab * 1024, send_sem.at[ab], recv_sem.at[ab])

    for load in loads[2:]:
        load.wait()

    y_swaps = []
    for ab in range(2):
        drain(recv, recv_sem.at[ab])

        def rows_of(t):
            top = [recv[pl.ds(ab * 1024 + t + half, CHIPS, stride=8), :] for half in range(2)]
            low = [recv[pl.ds(ab * 1024 + t + 2 + half, CHIPS, stride=8), :] for half in range(2)]
            return jnp.concatenate([jnp.concatenate(top, axis=1), jnp.concatenate(low, axis=1)], axis=0)

        u = rows_of(0).astype(BF16)
        a_buf[:, 0:256] = dot(first[:, 0:512], jnp.concatenate([u, u], axis=0))
        k_high, k_low = halves(rows_of(4))
        a_buf[:, 256:512] = dot(first[...], jnp.concatenate([k_high, k_high, k_low], axis=0))

        @pl.loop(0, 8)
        def _(i):
            rows = pl.ds(pl.multiple_of(i * 32, 32), 32)
            rows_im = pl.ds(pl.multiple_of(256 + i * 32, 32), 32)
            turn_re, turn_im = turn[rows, 0:256], turn[rows, 256:512]
            for which in range(2):
                cols = slice(which * 256, which * 256 + 256)
                re, im = a_buf[rows, cols], a_buf[rows_im, cols]
                to = pl.ds(pl.multiple_of(which * 256 + i * 32, 32), 32)
                high, low = halves(re * turn_re - im * turn_im)
                b_buf[to, 0:256], b_buf[to, 512:768] = high, low
                high, low = halves(re * turn_im + im * turn_re)
                b_buf[to, 256:512], b_buf[to, 768:1024] = high, low

        x_buf[...] = (
            dot(b_buf[:, 0:512], fwd[0:512, :]) + dot(b_buf[:, 512:1024], fwd[0:512, :])
            + dot(b_buf[:, 0:512], fwd[512:1024, :])
        )

        @pl.loop(0, 8)
        def _(i):
            rows = pl.ds(pl.multiple_of(i * 32, 32), 32)
            rows_k = pl.ds(pl.multiple_of(256 + i * 32, 32), 32)
            u_re, u_im = x_buf[rows, 0:256], x_buf[rows, 256:512]
            k_re, k_im = x_buf[rows_k, 0:256], x_buf[rows_k, 256:512]
            high, low = halves(u_re * k_re - u_im * k_im)
            p_buf[rows, 0:256], p_buf[rows, 512:768] = high, low
            high, low = halves(u_re * k_im + u_im * k_re)
            p_buf[rows, 256:512], p_buf[rows, 768:1024] = high, low

        c_buf[...] = (
            dot(p_buf[:, 0:512], bwd[0:512, :]) + dot(p_buf[:, 512:1024], bwd[0:512, :])
            + dot(p_buf[:, 0:512], bwd[512:1024, :])
        )

        @pl.loop(0, 8)
        def _(i):
            rows = pl.ds(pl.multiple_of(i * 32, 32), 32)
            turn_re, turn_im = turn[rows, 0:256], turn[rows, 256:512]
            re, im = c_buf[rows, 0:256], c_buf[rows, 256:512]
            for part, value in enumerate([re * turn_re + im * turn_im, im * turn_re - re * turn_im]):
                high, low = halves(value)
                for at, piece in ((0, high), (512, high), (1024, low)):
                    d_buf[pl.ds(pl.multiple_of(at + part * 256 + i * 32, 32), 32), :] = piece

        y_buf[ab] = dot(last[...], d_buf[...])

        swap = pltpu.make_async_remote_copy(
            src_ref=y_buf.at[ab, pl.ds(pl.multiple_of(other * 128, 128), 128)], dst_ref=y_sib.at[ab],
            send_sem=sib_send.at[2 + ab], recv_sem=sib_recv.at[2 + ab], device_id=sibling, device_id_type=MESH,
        )
        swap.start()
        y_swaps.append(swap)
        for half in range(2):
            y_send[pl.ds(4 * core + 2 * ab + half, CHIPS, stride=8), :] = y_buf[
                ab, pl.ds(pl.multiple_of(core * 128, 128), 128), half * 128 : half * 128 + 128
            ]

    for ab in range(2):
        y_swaps[ab].wait_recv()
        for half in range(2):
            y_send[pl.ds(4 * other + 2 * ab + half, CHIPS, stride=8), :] = y_sib[
                ab, :, half * 128 : half * 128 + 128
            ]
    spread(y_send, y_recv, 0, send_sem.at[2], recv_sem.at[2])
    drain(y_recv, recv_sem.at[2])

    for t in range(8):
        ch, half = t // 2 * 128, t % 2 * 128
        conv = y_recv[pl.ds(t, CHIPS, stride=8), :].T
        at = (slice(half, half + 128), slice(ch, ch + 128))
        mixed = (conv + byp_ref[:, ch : ch + 128] * wide[at]) * gate[at].astype(F32)
        out_ref[at] = mixed.astype(BF16)

    for swap in swaps + y_swaps:
        swap.wait_send()
    for ab in range(2):
        drain(send, send_sem.at[ab])
    drain(y_send, send_sem.at[2])


def on_device(consts, signal, gating, kernel, bypass):
    hbm, vmem = pl.BlockSpec(memory_space=pl.ANY), pl.BlockSpec(memory_space=pltpu.VMEM)
    v = pltpu.VMEM
    scratch = [
        v((256, 512), BF16), v((256, 512), BF16), v((256, 512), F32),
        *[v(c.shape, c.dtype) for c in consts],
        v((256, 512), F32), v((256, 256), F32), v((256, 256), F32),
        v((2048, 128), F32), v((2048, 128), F32),
        v((512, 512), F32), v((512, 1024), BF16), v((512, 512), F32), v((256, 1024), BF16), v((256, 512), F32),
        v((1536, 256), BF16), v((2, 256, 256), F32), v((2, 128, 256), F32), v((1024, 128), F32), v((1024, 128), F32),
        pltpu.SemaphoreType.DMA((8,)), pltpu.SemaphoreType.DMA((4,)), pltpu.SemaphoreType.DMA((4,)),
        pltpu.SemaphoreType.DMA((3,)), pltpu.SemaphoreType.DMA((3,)), pltpu.SemaphoreType.REGULAR,
    ]
    return pl.pallas_call(
        kernel_body,
        out_shape=jax.ShapeDtypeStruct((256, 512), BF16),
        in_specs=[hbm, hbm, hbm, vmem] + [hbm] * 5,
        out_specs=vmem,
        scratch_shapes=scratch,
        compiler_params=pltpu.CompilerParams(
            collective_id=0, has_side_effects=True, vmem_limit_bytes=48 * 1024 * 1024
        ),
        name="hyena",
    )(signal, gating, kernel, bypass.reshape(1, 512), *consts)


def solution(mesh):
    rows = P(("grp", "seq"), None)
    consts = tables()

    def whole(signal, gating, kernel, bypass):
        return jax.shard_map(
            functools.partial(on_device, [jnp.asarray(c) for c in consts]),
            mesh=mesh, in_specs=(rows, rows, rows, P()), out_specs=rows, check_vma=False,
        )(signal, gating, kernel, bypass)

    return whole
```

time: 857 us -> 71.7 us (0.08); the launches traced: 844 us -> 71.3 us
  waiting for transfers between devices: 400 us -> 0 us
  blocking collectives: 176 us -> 0 us
  starting transfers between devices: 100 us -> 0 us
  matrix products: 74.5 us -> 0 us
  local copies, waits for them, and re-layouts: 83.1 us -> 10.1 us
  Pallas kernels: 0 us -> 61.2 us
  other arithmetic: 9.19 us -> 0 us
    all_to_all x23 -> x0, waiting for transfers between devices: 400 us -> none  [the longest x1 26.8 us: spread_conv(): lax.all_to_all(twist_real, 'grp', split_axis=1, concat_axis=1, tiled=True)]
    all_to_all x7 -> x0, blocking collectives: 176 us -> none  [the longest x1 33.1 us: spread_conv(): lax.all_to_all(ker_imag, 'grp', split_axis=0, concat_axis=0, tiled=True)]
    all_to_all x23 -> x0, starting transfers between devices: 100 us -> none  [the longest x1 8.13 us: spread_conv(): lax.all_to_all(kspec_real.reshape(split_shape), 'grp', split_axis=1, conc...]
    dot_general x42 -> x0, matrix products: 74.5 us -> none  [the longest x6 12.2 us: transform(): jnp.einsum('kbm,bq->qkm', turned_imag, sin_second, precision=HIGHEST)]
    pallas_call x0 -> x1, Pallas kernels: none -> 61.2 us  [on_device(): pl.pallas_call(kernel_body, out_shape=jax.ShapeDtypeStruct((256, 512), BF...]
    all_to_all x20 -> x0, local copies, waits for them, and re-layouts: 27.2 us -> none  [the longest x1 2.8 us: spread_conv(): lax.all_to_all(sig_real, 'grp', split_axis=0, concat_axis=0, tiled=True)]
    reshape x10 -> x0, local copies, waits for them, and re-layouts: 17.1 us -> none  [the longest x3 7.07 us: transform(): final_real.reshape((length,) + trailing)]
    another operation x8 -> x0, local copies, waits for them, and re-layouts: 15.8 us -> none  [the longest x2 4.66 us: outer_forward(): real_part = real_part.reshape(2 * devices, piece_rows, channels)]
  transfers between devices with their start and end apart: 23 -> 0, of which waited for: 23 -> 0; matrix products, arithmetic and copies ran while one was open for 9% -> 0% of each run, Pallas kernels for 0% -> 0%
where the time goes in v1:
time: 71.7 us; the launch traced here: 71.3 us
  Pallas kernels  61.2 us (85%)
  local copies, waits for them, and re-layouts  10.1 us (14%)
    pallas_call x1, Pallas kernels, on_device(): pl.pallas_call(kernel_body, out_shape=jax.ShapeDtypeStruct((256, 512), BF...  61.2 us
    unnamed x19, local copies, waits for them, and re-layouts  10.1 us

profile of v1, /device:TPU:1, one launch (start us, length us, event | category | flops | bytes accessed | tf_op | source)
XLA Modules:
  0.0 71.3 jit_solution(3977257437830804199)
XLA Ops:
  0.0 0.0 copy-start
  0.0 1.2 %copy-done = bf16[1024,512]{1,0:T(8,128)(2,1)S(1)} copy-done((bf16[1024,512]{1,0:T(8,128)(2,1)S(1)}, bf16[1024,512]{1,0:T(8,128)(2,1)}, u32[]{:S(2)}) %copy-start) | copy-done | bytes 1048600
  1.2 0.0 copy-start.1
  1.2 1.2 %copy-done.1 = bf16[1024,512]{1,0:T(8,128)(2,1)S(1)} copy-done((bf16[1024,512]{1,0:T(8,128)(2,1)S(1)}, bf16[1024,512]{1,0:T(8,128)(2,1)}, u32[]{:S(2)}) %copy-start.1) | copy-done | bytes 1048600
  2.5 0.0 copy-start.2
  2.5 1.1 %copy-done.2 = bf16[256,1536]{1,0:T(8,128)(2,1)S(1)} copy-done((bf16[256,1536]{1,0:T(8,128)(2,1)S(1)}, bf16[256,1536]{1,0:T(8,128)(2,1)}, u32[]{:S(2)}) %copy-start.2) | copy-done | bytes 786456
  3.6 0.0 copy-start.3
  3.6 1.1 %copy-done.3 = bf16[512,768]{1,0:T(8,128)(2,1)S(1)} copy-done((bf16[512,768]{1,0:T(8,128)(2,1)S(1)}, bf16[512,768]{1,0:T(8,128)(2,1)}, u32[]{:S(2)}) %copy-start.3) | copy-done | bytes 786456
  4.7 0.0 copy-start.4
  4.7 1.0 %copy-done.4 = f32[256,512]{1,0:T(8,128)S(1)} copy-done((f32[256,512]{1,0:T(8,128)S(1)}, f32[256,512]{1,0:T(8,128)}, u32[]{:S(2)}) %copy-start.4) | copy-done | bytes 524312
  5.8 0.0 copy-start.5
  5.8 1.0 %copy-done.5 = f32[256,512]{1,0:T(8,128)S(1)} copy-done((f32[256,512]{1,0:T(8,128)S(1)}, f32[256,512]{1,0:T(8,128)}, u32[]{:S(2)}) %copy-start.5) | copy-done | bytes 524312
  6.8 0.0 copy-start.6
  6.8 0.9 %copy-done.6 = bf16[256,512]{1,0:T(8,128)(2,1)S(1)} copy-done((bf16[256,512]{1,0:T(8,128)(2,1)S(1)}, bf16[256,512]{1,0:T(8,128)(2,1)}, u32[]{:S(2)}) %copy-start.6) | copy-done | bytes 262168
  7.8 0.0 copy-start.7
  7.8 0.9 %copy-done.7 = bf16[256,512]{1,0:T(8,128)(2,1)S(1)} copy-done((bf16[256,512]{1,0:T(8,128)(2,1)S(1)}, bf16[256,512]{1,0:T(8,128)(2,1)}, u32[]{:S(2)}) %copy-start.7) | copy-done | bytes 262168
  8.7 0.0 copy-start.8
  8.7 0.7 copy-done.8
  9.4 61.2 %hyena.1 = bf16[256,512]{1,0:T(8,128)(2,1)S(1)} custom-call(bf16[256,512]{1,0:T(8,128)(2,1)S(1)} %copy-done.6, bf16[256,512]{1,0:T(8,128)(2,1)S(1)} %copy-done.7, f32[256,512]{1,0:T(8,128)S(1)} %copy-done.4, f32[1,512]{1,0:T(1,128)S(1)} %bitcast.1, bf16[512,768]{1,0:T(8,128)(2,1)S(1)} %copy-done.3, f32[256,512]{1,0:T(8,128)S(1)} %copy-done.5, ...), custom_call_target="tpu_custom_call" | custom-call | tf_op jit(solution)/shard_map/hyena/pallas_call | solution.py:263
  70.6 0.7 copy.11
Async XLA Ops:
  0.0 1.2 %copy-start = (bf16[1024,512]{1,0:T(8,128)(2,1)S(1)}, bf16[1024,512]{1,0:T(8,128)(2,1)}, u32[]{:S(2)}) copy-start(bf16[1024,512]{1,0:T(8,128)(2,1)} %constant.13.clone.bwd_hbm) | copy-start | bytes 3145732
  1.2 1.2 %copy-start.1 = (bf16[1024,512]{1,0:T(8,128)(2,1)S(1)}, bf16[1024,512]{1,0:T(8,128)(2,1)}, u32[]{:S(2)}) copy-start(bf16[1024,512]{1,0:T(8,128)(2,1)} %constant.12.clone.fwd_hbm) | copy-start | bytes 3145732
  2.5 1.1 %copy-start.2 = (bf16[256,1536]{1,0:T(8,128)(2,1)S(1)}, bf16[256,1536]{1,0:T(8,128)(2,1)}, u32[]{:S(2)}) copy-start(bf16[256,1536]{1,0:T(8,128)(2,1)} %constant.14.clone.last_hbm) | copy-start | bytes 2359300
  3.6 1.1 %copy-start.3 = (bf16[512,768]{1,0:T(8,128)(2,1)S(1)}, bf16[512,768]{1,0:T(8,128)(2,1)}, u32[]{:S(2)}) copy-start(bf16[512,768]{1,0:T(8,128)(2,1)} %constant.10.clone.first_hbm) | copy-start | bytes 2359300
  4.7 1.0 %copy-start.4 = (f32[256,512]{1,0:T(8,128)S(1)}, f32[256,512]{1,0:T(8,128)}, u32[]{:S(2)}) copy-start(f32[256,512]{1,0:T(8,128)} %ker_hbm.1) | copy-start | bytes 1572868
  5.8 1.0 %copy-start.5 = (f32[256,512]{1,0:T(8,128)S(1)}, f32[256,512]{1,0:T(8,128)}, u32[]{:S(2)}) copy-start(f32[256,512]{1,0:T(8,128)} %constant.11.clone.turn_hbm) | copy-start | bytes 1572868
  6.8 0.9 %copy-start.6 = (bf16[256,512]{1,0:T(8,128)(2,1)S(1)}, bf16[256,512]{1,0:T(8,128)(2,1)}, u32[]{:S(2)}) copy-start(bf16[256,512]{1,0:T(8,128)(2,1)} %sig_hbm.1) | copy-start | bytes 786436
  7.8 0.9 %copy-start.7 = (bf16[256,512]{1,0:T(8,128)(2,1)S(1)}, bf16[256,512]{1,0:T(8,128)(2,1)}, u32[]{:S(2)}) copy-start(bf16[256,512]{1,0:T(8,128)(2,1)} %gate_hbm.1) | copy-start | bytes 786436
  8.7 0.7 copy-start.8

commit v2 on v1

--- a/solution.py
+++ b/solution.py
@@ -125,40 +125,47 @@
             place(sib_k[rows, lanes], ab, 4 + 2 * other + half)
     pl.semaphore_wait(round_sem, 7)
 
-    def spread(source, target, base, sends, receives):
+    def spread(source, target, base, size, sends, receives):
         def step(i, carry):
-            to_z, to_x, to_y = (z + i % 8) % 8, (seq // 4 + i // 8 % 4) % 4, (seq % 4 + i // 32) % 4
-            to_seq = to_x * 4 + to_y
+            to_z = (z + i) & 7
+            to_seq = ((seq + (i >> 3 << 2)) & 12) | ((seq + (i >> 5)) & 3)
             to_chip = to_z * 16 + to_seq
             pltpu.make_async_remote_copy(
-                src_ref=source.at[pl.ds(pl.multiple_of(base + to_chip * 8, 8), 8)],
-                dst_ref=target.at[pl.ds(pl.multiple_of(base + chip * 8, 8), 8)],
+                src_ref=source.at[pl.ds(pl.multiple_of(base + to_chip * size, size), size)],
+                dst_ref=target.at[pl.ds(pl.multiple_of(base + chip * size, size), size)],
                 send_sem=sends, recv_sem=receives,
                 device_id=(to_z * 2 + core, to_seq), device_id_type=MESH,
             ).start()
             return carry
 
         lax.fori_loop(1, CHIPS, step, 0)
-        own = pl.ds(pl.multiple_of(base + chip * 8, 8), 8)
-        target[own, :] = source[own, :]
-
-    def drain(buffer, semaphore):
-        slabs = buffer.at[pl.ds(0, (CHIPS - 1) * 8)]
+
+    def drain(buffer, size, semaphore):
+        slabs = buffer.at[pl.ds(0, (CHIPS - 1) * size)]
         pltpu.make_async_copy(slabs, slabs, semaphore).wait()
 
     for ab in range(2):
-        spread(send, recv, ab * 1024, send_sem.at[ab], recv_sem.at[ab])
+        spread(send, recv, ab * 1024, 8, send_sem.at[ab], recv_sem.at[ab])
+        own = pl.ds(pl.multiple_of(ab * 1024 + chip * 8, 8), 8)
+        recv[own, :] = send[own, :]
 
     for load in loads[2:]:
         load.wait()
 
-    y_swaps = []
-    for ab in range(2):
-        drain(recv, recv_sem.at[ab])
+    def y_swap(ab):
+        return pltpu.make_async_remote_copy(
+            src_ref=y_buf.at[ab, pl.ds(pl.multiple_of(other * 128, 128), 128)], dst_ref=y_sib.at[ab],
+            send_sem=sib_send.at[2 + ab], recv_sem=sib_recv.at[2 + ab], device_id=sibling, device_id_type=MESH,
+        )
+
+    @pl.loop(0, 2)
+    def _(ab):
+        drain(recv, 8, recv_sem.at[ab])
+        base = pl.multiple_of(ab * 1024, 1024)
 
         def rows_of(t):
-            top = [recv[pl.ds(ab * 1024 + t + half, CHIPS, stride=8), :] for half in range(2)]
-            low = [recv[pl.ds(ab * 1024 + t + 2 + half, CHIPS, stride=8), :] for half in range(2)]
+            top = [recv[pl.ds(base + t + half, CHIPS, stride=8), :] for half in range(2)]
+            low = [recv[pl.ds(base + t + 2 + half, CHIPS, stride=8), :] for half in range(2)]
             return jnp.concatenate([jnp.concatenate(top, axis=1), jnp.concatenate(low, axis=1)], axis=0)
 
         u = rows_of(0).astype(BF16)
@@ -166,15 +173,13 @@
         k_high, k_low = halves(rows_of(4))
         a_buf[:, 256:512] = dot(first[...], jnp.concatenate([k_high, k_high, k_low], axis=0))
 
-        @pl.loop(0, 8)
-        def _(i):
-            rows = pl.ds(pl.multiple_of(i * 32, 32), 32)
-            rows_im = pl.ds(pl.multiple_of(256 + i * 32, 32), 32)
+        for i in range(8):
+            rows, rows_im = slice(i * 32, i * 32 + 32), slice(256 + i * 32, 288 + i * 32)
             turn_re, turn_im = turn[rows, 0:256], turn[rows, 256:512]
             for which in range(2):
                 cols = slice(which * 256, which * 256 + 256)
                 re, im = a_buf[rows, cols], a_buf[rows_im, cols]
-                to = pl.ds(pl.multiple_of(which * 256 + i * 32, 32), 32)
+                to = slice(which * 256 + i * 32, which * 256 + i * 32 + 32)
                 high, low = halves(re * turn_re - im * turn_im)
                 b_buf[to, 0:256], b_buf[to, 512:768] = high, low
                 high, low = halves(re * turn_im + im * turn_re)
@@ -185,10 +190,8 @@
             + dot(b_buf[:, 0:512], fwd[512:1024, :])
         )
 
-        @pl.loop(0, 8)
-        def _(i):
-            rows = pl.ds(pl.multiple_of(i * 32, 32), 32)
-            rows_k = pl.ds(pl.multiple_of(256 + i * 32, 32), 32)
+        for i in range(8):
+            rows, rows_k = slice(i * 32, i * 32 + 32), slice(256 + i * 32, 288 + i * 32)
             u_re, u_im = x_buf[rows, 0:256], x_buf[rows, 256:512]
             k_re, k_im = x_buf[rows_k, 0:256], x_buf[rows_k, 256:512]
             high, low = halves(u_re * k_re - u_im * k_im)
@@ -201,54 +204,49 @@
             + dot(p_buf[:, 0:512], bwd[512:1024, :])
         )
 
-        @pl.loop(0, 8)
-        def _(i):
-            rows = pl.ds(pl.multiple_of(i * 32, 32), 32)
+        for i in range(8):
+            rows = slice(i * 32, i * 32 + 32)
             turn_re, turn_im = turn[rows, 0:256], turn[rows, 256:512]
             re, im = c_buf[rows, 0:256], c_buf[rows, 256:512]
             for part, value in enumerate([re * turn_re + im * turn_im, im * turn_re - re * turn_im]):
                 high, low = halves(value)
                 for at, piece in ((0, high), (512, high), (1024, low)):
-                    d_buf[pl.ds(pl.multiple_of(at + part * 256 + i * 32, 32), 32), :] = piece
-
-        y_buf[ab] = dot(last[...], d_buf[...])
-
-        swap = pltpu.make_async_remote_copy(
-            src_ref=y_buf.at[ab, pl.ds(pl.multiple_of(other * 128, 128), 128)], dst_ref=y_sib.at[ab],
-            send_sem=sib_send.at[2 + ab], recv_sem=sib_recv.at[2 + ab], device_id=sibling, device_id_type=MESH,
-        )
+                    d_buf[at + part * 256 + i * 32 : at + part * 256 + i * 32 + 32, :] = piece
+
+        near = pl.ds(pl.multiple_of(core * 128, 128), 128)
+        away = pl.ds(pl.multiple_of(other * 128, 128), 128)
+        y_buf[ab, away] = dot(last[away, :], d_buf[...])
+        swap = y_swap(ab)
         swap.start()
-        y_swaps.append(swap)
-        for half in range(2):
-            y_send[pl.ds(4 * core + 2 * ab + half, CHIPS, stride=8), :] = y_buf[
-                ab, pl.ds(pl.multiple_of(core * 128, 128), 128), half * 128 : half * 128 + 128
-            ]
-
-    for ab in range(2):
-        y_swaps[ab].wait_recv()
-        for half in range(2):
-            y_send[pl.ds(4 * other + 2 * ab + half, CHIPS, stride=8), :] = y_sib[
-                ab, :, half * 128 : half * 128 + 128
-            ]
-    spread(y_send, y_recv, 0, send_sem.at[2], recv_sem.at[2])
-    drain(y_recv, recv_sem.at[2])
-
-    for t in range(8):
-        ch, half = t // 2 * 128, t % 2 * 128
-        conv = y_recv[pl.ds(t, CHIPS, stride=8), :].T
-        at = (slice(half, half + 128), slice(ch, ch + 128))
-        mixed = (conv + byp_ref[:, ch : ch + 128] * wide[at]) * gate[at].astype(F32)
-        out_ref[at] = mixed.astype(BF16)
-
-    for swap in swaps + y_swaps:
-        swap.wait_send()
-    for ab in range(2):
-        drain(send, send_sem.at[ab])
-    drain(y_send, send_sem.at[2])
+        y_buf[ab, near] = dot(last[near, :], d_buf[...])
+        at = pl.multiple_of(ab * 512, 512)
+        for half in range(2):
+            y_send[pl.ds(at + 2 * core + half, CHIPS, stride=4), :] = y_buf[ab, near, half * 128 : half * 128 + 128]
+        swap.wait_recv()
+        for half in range(2):
+            y_send[pl.ds(at + 2 * other + half, CHIPS, stride=4), :] = y_sib[ab, :, half * 128 : half * 128 + 128]
+        spread(y_send, y_recv, at, 4, send_sem.at[2 + ab], recv_sem.at[2 + ab])
+        own = pl.ds(pl.multiple_of(at + chip * 4, 4), 4)
+        y_recv[own, :] = y_send[own, :]
+
+    for ab in range(2):
+        drain(y_recv, 4, recv_sem.at[2 + ab])
+        for t in range(4):
+            ch, half = t // 2 * 256 + ab * 128, t % 2 * 128
+            conv = y_recv[pl.ds(ab * 512 + t, CHIPS, stride=4), :].T
+            at = (slice(half, half + 128), slice(ch, ch + 128))
+            mixed = (conv + byp_ref[:, ch : ch + 128] * wide[at]) * gate[at].astype(F32)
+            out_ref[at] = mixed.astype(BF16)
+
+    for ab in range(2):
+        swaps[ab].wait_send()
+        y_swap(ab).wait_send()
+        drain(send, 8, send_sem.at[ab])
+        drain(y_send, 4, send_sem.at[2 + ab])
 
 
 def on_device(consts, signal, gating, kernel, bypass):
-    hbm, vmem = pl.BlockSpec(memory_space=pl.ANY), pl.BlockSpec(memory_space=pltpu.VMEM)
+    hbm, vmem = pl.BlockSpec(memory_space=pltpu.HBM), pl.BlockSpec(memory_space=pltpu.VMEM)
     v = pltpu.VMEM
     scratch = [
         v((256, 512), BF16), v((256, 512), BF16), v((256, 512), F32),
@@ -258,7 +256,7 @@
         v((512, 512), F32), v((512, 1024), BF16), v((512, 512), F32), v((256, 1024), BF16), v((256, 512), F32),
         v((1536, 256), BF16), v((2, 256, 256), F32), v((2, 128, 256), F32), v((1024, 128), F32), v((1024, 128), F32),
         pltpu.SemaphoreType.DMA((8,)), pltpu.SemaphoreType.DMA((4,)), pltpu.SemaphoreType.DMA((4,)),
-        pltpu.SemaphoreType.DMA((3,)), pltpu.SemaphoreType.DMA((3,)), pltpu.SemaphoreType.REGULAR,
+        pltpu.SemaphoreType.DMA((4,)), pltpu.SemaphoreType.DMA((4,)), pltpu.SemaphoreType.REGULAR,
     ]
     return pl.pallas_call(
         kernel_body,
@@ -267,7 +265,7 @@
         out_specs=vmem,
         scratch_shapes=scratch,
         compiler_params=pltpu.CompilerParams(
-            collective_id=0, has_side_effects=True, vmem_limit_bytes=48 * 1024 * 1024
+            collective_id=0, has_side_effects=True, vmem_limit_bytes=63 * 1024 * 1024
         ),
         name="hyena",
     )(signal, gating, kernel, bypass.reshape(1, 512), *consts)

time: 71.7 us -> 58.3 us (0.81)
  local copies, waits for them, and re-layouts: 10.1 us -> 1.67 us
  Pallas kernels: 61.2 us -> 56.5 us
    unnamed x19 -> x1, local copies, waits for them, and re-layouts: 10.1 us -> 1.67 us
    pallas_call x1, Pallas kernels: 61.2 us -> 56.5 us  [on_device(): pl.pallas_call(kernel_body, out_shape=jax.ShapeDtypeStruct((256, 512), BF...]
where the time goes in v2:
time: 58.3 us; the launch traced here: 58.1 us
  Pallas kernels  56.5 us (97%)
  local copies, waits for them, and re-layouts  1.67 us (3%)
    pallas_call x1, Pallas kernels, on_device(): pl.pallas_call(kernel_body, out_shape=jax.ShapeDtypeStruct((256, 512), BF...  56.5 us
    unnamed x1, local copies, waits for them, and re-layouts  1.67 us

profile of v2, /device:TPU:1, one launch (start us, length us, event | category | flops | bytes accessed | tf_op | source)
XLA Modules:
  0.0 58.1 jit_solution(7963976227489660128)
XLA Ops:
  0.0 56.5 %hyena.1 = bf16[256,512]{1,0:T(8,128)(2,1)} custom-call(bf16[256,512]{1,0:T(8,128)(2,1)} %sig_hbm.1, bf16[256,512]{1,0:T(8,128)(2,1)} %gate_hbm.1, f32[256,512]{1,0:T(8,128)} %ker_hbm.1, f32[1,512]{1,0:T(1,128)} %bitcast.1, bf16[512,768]{1,0:T(8,128)(2,1)} %constant.10.clone.first_hbm, f32[256,512]{1,0:T(8,128)} %constant.11.clone.turn_hbm, ...), custom_call_target="tpu_custom_call" | custom-call | tf_op jit(solution)/shard_map/hyena/pallas_call | solution.py:261
  56.5 1.7 %copy.11 = bf16[256,512]{1,0:T(8,128)(2,1)} copy(bf16[256,512]{1,0:T(8,128)(2,1)} %hyena.1) | data formatting | bytes 524288

commit v3 on v2

--- a/solution.py
+++ b/solution.py
@@ -17,6 +17,15 @@
 TOKENS = 65536
 
 
+def hops(offset):
+    dz, dx, dy = offset
+    return min(dz, 8 - dz) + min(dx, 4 - dx) + min(dy, 4 - dy)
+
+
+OFFSETS = [(dz, dx, dy) for dx in range(4) for dy in range(4) for dz in range(8)]
+FAR_FIRST = sorted(OFFSETS[1:], key=lambda offset: -hops(offset))
+
+
 def split_table(table):
     high = table.astype(ml_dtypes.bfloat16)
     low = (table - high.astype(np.float64)).astype(ml_dtypes.bfloat16)
@@ -58,9 +67,9 @@
 
 
 def kernel_body(
-    sig_hbm, gate_hbm, ker_hbm, byp_ref, first_hbm, turn_hbm, fwd_hbm, bwd_hbm, last_hbm,
+    sig_hbm, gate_hbm, ker_hbm, byp_hbm, first_hbm, turn_hbm, fwd_hbm, bwd_hbm, last_hbm,
     out_ref,
-    sig, gate, ker, first, turn, fwd, bwd, last,
+    sig, gate, ker, byp, first, turn, fwd, bwd, last,
     wide, sib_u, sib_k, send, recv, a_buf, b_buf, x_buf, p_buf, c_buf, d_buf, y_buf, y_sib, y_send, y_recv,
     load_sem, sib_send, sib_recv, send_sem, recv_sem, round_sem,
 ):
@@ -71,18 +80,21 @@
     sibling = (z * 2 + other, seq)
 
     barrier = pltpu.get_barrier_semaphore()
+    in_line = (4, 3, 5, 2, 6, 1, 7)
+    for dz in in_line:
+        pl.semaphore_signal(barrier, inc=1, device_id=(((z + dz) & 7) * 2 + core, seq), device_id_type=MESH)
+    for dz, dx, dy in FAR_FIRST:
+        if dz == 0:
+            mate = ((seq + 4 * dx) & 12) | ((seq + dy) & 3)
+            pl.semaphore_signal(barrier, inc=1, device_id=(grp, mate), device_id_type=MESH)
     pl.semaphore_signal(barrier, inc=1, device_id=sibling, device_id_type=MESH)
-    for j in range(1, 8):
-        pl.semaphore_signal(barrier, inc=1, device_id=((z + j) % 8 * 2 + core, seq), device_id_type=MESH)
-    for j in range(1, 16):
-        pl.semaphore_signal(barrier, inc=1, device_id=(grp, (seq + j) % 16), device_id_type=MESH)
 
     loads = [
         pltpu.make_async_copy(source, target, load_sem.at[i])
         for i, (source, target) in enumerate(
             [
                 (ker_hbm, ker), (sig_hbm, sig), (first_hbm, first), (turn_hbm, turn),
-                (fwd_hbm, fwd), (bwd_hbm, bwd), (last_hbm, last), (gate_hbm, gate),
+                (fwd_hbm, fwd), (bwd_hbm, bwd), (last_hbm, last), (gate_hbm, gate), (byp_hbm, byp),
             ]
         )
     ]
@@ -104,31 +116,29 @@
     ]
     for swap in swaps:
         swap.start()
-    for j in range(1, 8):
-        pl.semaphore_signal(round_sem, inc=1, device_id=((z + j) % 8 * 2 + core, seq), device_id_type=MESH)
+    for dz in in_line:
+        pl.semaphore_signal(round_sem, inc=1, device_id=(((z + dz) & 7) * 2 + core, seq), device_id_type=MESH)
 
     def place(block, ab, start):
         send[pl.ds(ab * 1024 + start, CHIPS, stride=8), :] = block.T
 
-    for ab in range(2):
+    def place_near(ab):
         for half in range(2):
             rows = pl.ds(half * 128, 128)
             lanes = pl.ds(near_lanes + ab * 128, 128)
+            place(ker[rows, lanes], ab, 4 + 2 * core + half)
             place(wide[rows, lanes], ab, 2 * core + half)
-            place(ker[rows, lanes], ab, 4 + 2 * core + half)
-    swaps[0].wait_recv()
-    swaps[1].wait_recv()
-    for ab in range(2):
+
+    def place_sibling(ab, which):
+        source, at = ((sib_k, 4), (sib_u, 0))[which]
         for half in range(2):
             rows, lanes = pl.ds(half * 128, 128), pl.ds(ab * 128, 128)
-            place(sib_u[rows, lanes], ab, 2 * other + half)
-            place(sib_k[rows, lanes], ab, 4 + 2 * other + half)
-    pl.semaphore_wait(round_sem, 7)
+            place(source[rows, lanes], ab, at + 2 * other + half)
 
     def spread(source, target, base, size, sends, receives):
-        def step(i, carry):
-            to_z = (z + i) & 7
-            to_seq = ((seq + (i >> 3 << 2)) & 12) | ((seq + (i >> 5)) & 3)
+        for dz, dx, dy in FAR_FIRST:
+            to_z = (z + dz) & 7
+            to_seq = ((seq + 4 * dx) & 12) | ((seq + dy) & 3)
             to_chip = to_z * 16 + to_seq
             pltpu.make_async_remote_copy(
                 src_ref=source.at[pl.ds(pl.multiple_of(base + to_chip * size, size), size)],
@@ -136,18 +146,26 @@
                 send_sem=sends, recv_sem=receives,
                 device_id=(to_z * 2 + core, to_seq), device_id_type=MESH,
             ).start()
-            return carry
-
-        lax.fori_loop(1, CHIPS, step, 0)
 
     def drain(buffer, size, semaphore):
         slabs = buffer.at[pl.ds(0, (CHIPS - 1) * size)]
         pltpu.make_async_copy(slabs, slabs, semaphore).wait()
 
-    for ab in range(2):
+    def send_slabs(ab):
         spread(send, recv, ab * 1024, 8, send_sem.at[ab], recv_sem.at[ab])
         own = pl.ds(pl.multiple_of(ab * 1024 + chip * 8, 8), 8)
         recv[own, :] = send[own, :]
+
+    place_near(0)
+    place_near(1)
+    for which in range(2):
+        swaps[which].wait_recv()
+        place_sibling(0, which)
+    pl.semaphore_wait(round_sem, 7)
+    send_slabs(0)
+    for which in range(2):
+        place_sibling(1, which)
+    send_slabs(1)
 
     for load in loads[2:]:
         load.wait()
@@ -213,12 +231,18 @@
                 for at, piece in ((0, high), (512, high), (1024, low)):
                     d_buf[at + part * 256 + i * 32 : at + part * 256 + i * 32 + 32, :] = piece
 
+        factor = byp[core * 256 + ab * CHIPS + chip]
+
+        def u_part(which):
+            part = [recv[pl.ds(base + 2 * which + half, CHIPS, stride=8), :] for half in range(2)]
+            return jnp.concatenate(part, axis=1)
+
         near = pl.ds(pl.multiple_of(core * 128, 128), 128)
         away = pl.ds(pl.multiple_of(other * 128, 128), 128)
-        y_buf[ab, away] = dot(last[away, :], d_buf[...])
+        y_buf[ab, away] = dot(last[away, :], d_buf[...]) + factor * u_part(other)
         swap = y_swap(ab)
         swap.start()
-        y_buf[ab, near] = dot(last[near, :], d_buf[...])
+        y_buf[ab, near] = dot(last[near, :], d_buf[...]) + factor * u_part(core)
         at = pl.multiple_of(ab * 512, 512)
         for half in range(2):
             y_send[pl.ds(at + 2 * core + half, CHIPS, stride=4), :] = y_buf[ab, near, half * 128 : half * 128 + 128]
@@ -233,10 +257,9 @@
         drain(y_recv, 4, recv_sem.at[2 + ab])
         for t in range(4):
             ch, half = t // 2 * 256 + ab * 128, t % 2 * 128
-            conv = y_recv[pl.ds(ab * 512 + t, CHIPS, stride=4), :].T
+            mixed = y_recv[pl.ds(ab * 512 + t, CHIPS, stride=4), :].T
             at = (slice(half, half + 128), slice(ch, ch + 128))
-            mixed = (conv + byp_ref[:, ch : ch + 128] * wide[at]) * gate[at].astype(F32)
-            out_ref[at] = mixed.astype(BF16)
+            out_ref[at] = (mixed * gate[at].astype(F32)).astype(BF16)
 
     for ab in range(2):
         swaps[ab].wait_send()
@@ -249,26 +272,26 @@
     hbm, vmem = pl.BlockSpec(memory_space=pltpu.HBM), pl.BlockSpec(memory_space=pltpu.VMEM)
     v = pltpu.VMEM
     scratch = [
-        v((256, 512), BF16), v((256, 512), BF16), v((256, 512), F32),
+        v((256, 512), BF16), v((256, 512), BF16), v((256, 512), F32), pltpu.SMEM((512,), F32),
         *[v(c.shape, c.dtype) for c in consts],
         v((256, 512), F32), v((256, 256), F32), v((256, 256), F32),
         v((2048, 128), F32), v((2048, 128), F32),
         v((512, 512), F32), v((512, 1024), BF16), v((512, 512), F32), v((256, 1024), BF16), v((256, 512), F32),
         v((1536, 256), BF16), v((2, 256, 256), F32), v((2, 128, 256), F32), v((1024, 128), F32), v((1024, 128), F32),
-        pltpu.SemaphoreType.DMA((8,)), pltpu.SemaphoreType.DMA((4,)), pltpu.SemaphoreType.DMA((4,)),
+        pltpu.SemaphoreType.DMA((9,)), pltpu.SemaphoreType.DMA((4,)), pltpu.SemaphoreType.DMA((4,)),
         pltpu.SemaphoreType.DMA((4,)), pltpu.SemaphoreType.DMA((4,)), pltpu.SemaphoreType.REGULAR,
     ]
     return pl.pallas_call(
         kernel_body,
         out_shape=jax.ShapeDtypeStruct((256, 512), BF16),
-        in_specs=[hbm, hbm, hbm, vmem] + [hbm] * 5,
+        in_specs=[hbm] * 9,
         out_specs=vmem,
         scratch_shapes=scratch,
         compiler_params=pltpu.CompilerParams(
             collective_id=0, has_side_effects=True, vmem_limit_bytes=63 * 1024 * 1024
         ),
         name="hyena",
-    )(signal, gating, kernel, bypass.reshape(1, 512), *consts)
+    )(signal, gating, kernel, bypass, *consts)
 
 
 def solution(mesh):

time: 58.3 us -> 56.2 us (0.964)
  Pallas kernels: 56.5 us -> 54.4 us
    pallas_call x1, Pallas kernels: 56.5 us -> 54.4 us  [on_device(): pl.pallas_call(kernel_body, out_shape=jax.ShapeDtypeStruct((256, 512), BF...]
where the time goes in v3:
time: 56.2 us; the launch traced here: 56.1 us
  Pallas kernels  54.4 us (97%)
  local copies, waits for them, and re-layouts  1.67 us (3%)
    pallas_call x1, Pallas kernels, on_device(): pl.pallas_call(kernel_body, out_shape=jax.ShapeDtypeStruct((256, 512), BF...  54.4 us
    unnamed x1, local copies, waits for them, and re-layouts  1.67 us

profile of v3, /device:TPU:1, one launch (start us, length us, event | category | flops | bytes accessed | tf_op | source)
XLA Modules:
  0.0 56.1 jit_solution(4541715182726545790)
XLA Ops:
  0.0 54.4 %hyena.1 = bf16[256,512]{1,0:T(8,128)(2,1)} custom-call(bf16[256,512]{1,0:T(8,128)(2,1)} %sig_hbm.1, bf16[256,512]{1,0:T(8,128)(2,1)} %gate_hbm.1, f32[256,512]{1,0:T(8,128)} %ker_hbm.1, f32[512]{0:T(512)} %byp_hbm.1, bf16[512,768]{1,0:T(8,128)(2,1)} %constant.10.clone.first_hbm, f32[256,512]{1,0:T(8,128)} %constant.11.clone.turn_hbm, ...), custom_call_target="tpu_custom_call" | custom-call | tf_op jit(solution)/shard_map/hyena/pallas_call | solution.py:284
  54.4 1.7 %copy.11 = bf16[256,512]{1,0:T(8,128)(2,1)} copy(bf16[256,512]{1,0:T(8,128)(2,1)} %hyena.1) | data formatting | bytes 524288

commit v4 on v3

--- a/solution.py
+++ b/solution.py
@@ -40,7 +40,9 @@
     quarter = 4 * index - 1
 
     first = 2.0 * np.pi / 1024 * (quarter[:, None] * n1[None, :] % 1024)
-    first_high, first_low = split_table(np.concatenate([np.cos(first), -np.sin(first)], axis=0))
+    halved = first.reshape(2, 1, 128, 256)
+    first_rows = np.concatenate([np.cos(halved), -np.sin(halved)], axis=1).reshape(512, 256)
+    first_high, first_low = split_table(first_rows)
     first_all = np.concatenate([first_high, first_low, first_high], axis=1)
 
     turn = 2.0 * np.pi / (4 * TOKENS) * (quarter[:, None] * index[None, :] % (4 * TOKENS))
@@ -187,49 +189,67 @@
             return jnp.concatenate([jnp.concatenate(top, axis=1), jnp.concatenate(low, axis=1)], axis=0)
 
         u = rows_of(0).astype(BF16)
-        a_buf[:, 0:256] = dot(first[:, 0:512], jnp.concatenate([u, u], axis=0))
+        u_twice = jnp.concatenate([u, u], axis=0)
         k_high, k_low = halves(rows_of(4))
-        a_buf[:, 256:512] = dot(first[...], jnp.concatenate([k_high, k_high, k_low], axis=0))
-
-        for i in range(8):
-            rows, rows_im = slice(i * 32, i * 32 + 32), slice(256 + i * 32, 288 + i * 32)
-            turn_re, turn_im = turn[rows, 0:256], turn[rows, 256:512]
-            for which in range(2):
-                cols = slice(which * 256, which * 256 + 256)
-                re, im = a_buf[rows, cols], a_buf[rows_im, cols]
-                to = slice(which * 256 + i * 32, which * 256 + i * 32 + 32)
-                high, low = halves(re * turn_re - im * turn_im)
-                b_buf[to, 0:256], b_buf[to, 512:768] = high, low
-                high, low = halves(re * turn_im + im * turn_re)
-                b_buf[to, 256:512], b_buf[to, 768:1024] = high, low
-
-        x_buf[...] = (
-            dot(b_buf[:, 0:512], fwd[0:512, :]) + dot(b_buf[:, 512:1024], fwd[0:512, :])
-            + dot(b_buf[:, 0:512], fwd[512:1024, :])
-        )
-
-        for i in range(8):
-            rows, rows_k = slice(i * 32, i * 32 + 32), slice(256 + i * 32, 288 + i * 32)
-            u_re, u_im = x_buf[rows, 0:256], x_buf[rows, 256:512]
-            k_re, k_im = x_buf[rows_k, 0:256], x_buf[rows_k, 256:512]
-            high, low = halves(u_re * k_re - u_im * k_im)
-            p_buf[rows, 0:256], p_buf[rows, 512:768] = high, low
-            high, low = halves(u_re * k_im + u_im * k_re)
-            p_buf[rows, 256:512], p_buf[rows, 768:1024] = high, low
-
-        c_buf[...] = (
-            dot(p_buf[:, 0:512], bwd[0:512, :]) + dot(p_buf[:, 512:1024], bwd[0:512, :])
-            + dot(p_buf[:, 0:512], bwd[512:1024, :])
-        )
-
-        for i in range(8):
-            rows = slice(i * 32, i * 32 + 32)
-            turn_re, turn_im = turn[rows, 0:256], turn[rows, 256:512]
-            re, im = c_buf[rows, 0:256], c_buf[rows, 256:512]
-            for part, value in enumerate([re * turn_re + im * turn_im, im * turn_re - re * turn_im]):
-                high, low = halves(value)
-                for at, piece in ((0, high), (512, high), (1024, low)):
-                    d_buf[at + part * 256 + i * 32 : at + part * 256 + i * 32 + 32, :] = piece
+        k_thrice = jnp.concatenate([k_high, k_high, k_low], axis=0)
+
+        def columns(part):
+            at = slice(part * 256, part * 256 + 256)
+            a_buf[at, 0:256] = dot(first[at, 0:512], u_twice)
+            a_buf[at, 256:512] = dot(first[at, :], k_thrice)
+
+        def twist(part):
+            for i in range(0, 128, 32):
+                re_rows = slice(part * 256 + i, part * 256 + i + 32)
+                im_rows = slice(part * 256 + 128 + i, part * 256 + 160 + i)
+                rows = slice(part * 128 + i, part * 128 + i + 32)
+                turn_re, turn_im = turn[rows, 0:256], turn[rows, 256:512]
+                for which, to in enumerate((re_rows, im_rows)):
+                    cols = slice(which * 256, which * 256 + 256)
+                    re, im = a_buf[re_rows, cols], a_buf[im_rows, cols]
+                    high, low = halves(re * turn_re - im * turn_im)
+                    b_buf[to, 0:256], b_buf[to, 512:768] = high, low
+                    high, low = halves(re * turn_im + im * turn_re)
+                    b_buf[to, 256:512], b_buf[to, 768:1024] = high, low
+
+        def three(data, table, rows):
+            high, low = data[rows, 0:512], data[rows, 512:1024]
+            return dot(high, table[0:512, :]) + dot(low, table[0:512, :]) + dot(high, table[512:1024, :])
+
+        def product(part):
+            for i in range(0, 128, 32):
+                u_rows = slice(part * 256 + i, part * 256 + i + 32)
+                k_rows = slice(part * 256 + 128 + i, part * 256 + 160 + i)
+                to = slice(part * 128 + i, part * 128 + i + 32)
+                u_re, u_im = x_buf[u_rows, 0:256], x_buf[u_rows, 256:512]
+                k_re, k_im = x_buf[k_rows, 0:256], x_buf[k_rows, 256:512]
+                high, low = halves(u_re * k_re - u_im * k_im)
+                p_buf[to, 0:256], p_buf[to, 512:768] = high, low
+                high, low = halves(u_re * k_im + u_im * k_re)
+                p_buf[to, 256:512], p_buf[to, 768:1024] = high, low
+
+        def untwist(part):
+            for i in range(part * 128, part * 128 + 128, 32):
+                rows = slice(i, i + 32)
+                turn_re, turn_im = turn[rows, 0:256], turn[rows, 256:512]
+                re, im = c_buf[rows, 0:256], c_buf[rows, 256:512]
+                for at, value in ((i, re * turn_re + im * turn_im), (256 + i, im * turn_re - re * turn_im)):
+                    high, low = halves(value)
+                    d_buf[at : at + 32, :], d_buf[512 + at : 544 + at, :] = high, high
+                    d_buf[1024 + at : 1056 + at, :] = low
+
+        columns(0)
+        columns(1)
+        twist(0)
+        x_buf[0:256, :] = three(b_buf, fwd, slice(0, 256))
+        twist(1)
+        x_buf[256:512, :] = three(b_buf, fwd, slice(256, 512))
+        product(0)
+        c_buf[0:128, :] = three(p_buf, bwd, slice(0, 128))
+        product(1)
+        c_buf[128:256, :] = three(p_buf, bwd, slice(128, 256))
+        untwist(0)
+        untwist(1)
 
         factor = byp[core * 256 + ab * CHIPS + chip]
 
@@ -281,17 +301,18 @@
         pltpu.SemaphoreType.DMA((9,)), pltpu.SemaphoreType.DMA((4,)), pltpu.SemaphoreType.DMA((4,)),
         pltpu.SemaphoreType.DMA((4,)), pltpu.SemaphoreType.DMA((4,)), pltpu.SemaphoreType.REGULAR,
     ]
+    operands = [pltpu.with_memory_space_constraint(x, pltpu.HBM) for x in (signal, gating, kernel, bypass, *consts)]
     return pl.pallas_call(
         kernel_body,
-        out_shape=jax.ShapeDtypeStruct((256, 512), BF16),
+        out_shape=pltpu.VMEM((256, 512), BF16),
         in_specs=[hbm] * 9,
         out_specs=vmem,
         scratch_shapes=scratch,
         compiler_params=pltpu.CompilerParams(
-            collective_id=0, has_side_effects=True, vmem_limit_bytes=63 * 1024 * 1024
+            collective_id=0, has_side_effects=True, vmem_limit_bytes=48 * 1024 * 1024
         ),
         name="hyena",
-    )(signal, gating, kernel, bypass, *consts)
+    )(*operands)
 
 
 def solution(mesh):

time: 56.2 us -> 54 us (0.961)
  Pallas kernels: 54.4 us -> 53.2 us
  local copies, waits for them, and re-layouts: 1.67 us -> 0.71 us
    pallas_call x1, Pallas kernels: 54.4 us -> 53.2 us  [on_device(): pl.pallas_call(kernel_body, out_shape=pltpu.VMEM((256, 512), BF16), in_sp...]
    unnamed x1, local copies, waits for them, and re-layouts: 1.67 us -> 0.71 us
where the time goes in v4:
time: 54 us; the launch traced here: 53.9 us
  Pallas kernels  53.2 us (99%)
  local copies, waits for them, and re-layouts  0.71 us (1%)
    pallas_call x1, Pallas kernels, on_device(): pl.pallas_call(kernel_body, out_shape=pltpu.VMEM((256, 512), BF16), in_sp...  53.2 us

profile of v4, /device:TPU:1, one launch (start us, length us, event | category | flops | bytes accessed | tf_op | source)
XLA Modules:
  0.0 53.9 jit_solution(14661250216124031409)
XLA Ops:
  0.0 53.2 %hyena.1 = bf16[256,512]{1,0:T(8,128)(2,1)S(1)} custom-call(bf16[256,512]{1,0:T(8,128)(2,1)} %sig_hbm.1, bf16[256,512]{1,0:T(8,128)(2,1)} %gate_hbm.1, f32[256,512]{1,0:T(8,128)} %ker_hbm.1, f32[512]{0:T(512)} %byp_hbm.1, bf16[512,768]{1,0:T(8,128)(2,1)} %constant.10.clone.first_hbm, f32[256,512]{1,0:T(8,128)} %constant.11.clone.turn_hbm, ...), custom_call_target="tpu_custom_call" | custom-call | tf_op jit(solution)/shard_map/hyena/pallas_call | solution.py:305
  53.2 0.7 %copy.11 = bf16[256,512]{1,0:T(8,128)(2,1)} copy(bf16[256,512]{1,0:T(8,128)(2,1)S(1)} %hyena.1) | data formatting | bytes 524288

commit v5 on v4

--- a/solution.py
+++ b/solution.py
@@ -24,6 +24,7 @@
 
 OFFSETS = [(dz, dx, dy) for dx in range(4) for dy in range(4) for dz in range(8)]
 FAR_FIRST = sorted(OFFSETS[1:], key=lambda offset: -hops(offset))
+PLANES = (1, 7, 2, 6, 3, 5, 4)
 
 
 def split_table(table):
@@ -73,23 +74,13 @@
     out_ref,
     sig, gate, ker, byp, first, turn, fwd, bwd, last,
     wide, sib_u, sib_k, send, recv, a_buf, b_buf, x_buf, p_buf, c_buf, d_buf, y_buf, y_sib, y_send, y_recv,
-    load_sem, sib_send, sib_recv, send_sem, recv_sem, round_sem,
+    load_sem, sib_send, sib_recv, send_sem, recv_sem, plane_sem,
 ):
     grp, seq = lax.axis_index("grp"), lax.axis_index("seq")
     z, core = grp // 2, grp % 2
     other = 1 - core
     chip = z * 16 + seq
     sibling = (z * 2 + other, seq)
-
-    barrier = pltpu.get_barrier_semaphore()
-    in_line = (4, 3, 5, 2, 6, 1, 7)
-    for dz in in_line:
-        pl.semaphore_signal(barrier, inc=1, device_id=(((z + dz) & 7) * 2 + core, seq), device_id_type=MESH)
-    for dz, dx, dy in FAR_FIRST:
-        if dz == 0:
-            mate = ((seq + 4 * dx) & 12) | ((seq + dy) & 3)
-            pl.semaphore_signal(barrier, inc=1, device_id=(grp, mate), device_id_type=MESH)
-    pl.semaphore_signal(barrier, inc=1, device_id=sibling, device_id_type=MESH)
 
     loads = [
         pltpu.make_async_copy(source, target, load_sem.at[i])
@@ -100,13 +91,28 @@
             ]
         )
     ]
-    for load in loads:
+    for load in loads[:2]:
+        load.start()
+
+    barrier = pltpu.get_barrier_semaphore()
+    pl.semaphore_signal(barrier, inc=1, device_id=sibling, device_id_type=MESH)
+    for dz, dx, dy in FAR_FIRST:
+        if dz == 0:
+            mate = ((seq + 4 * dx) & 12) | ((seq + dy) & 3)
+            pl.semaphore_signal(barrier, inc=1, device_id=(grp, mate), device_id_type=MESH)
+    for dz in PLANES:
+        pl.semaphore_signal(barrier, inc=1, device_id=(((z + dz) & 7) * 2 + core, seq), device_id_type=MESH)
+    for load in loads[2:]:
         load.start()
     loads[0].wait()
     loads[1].wait()
     wide[...] = sig[...].astype(F32)
 
     pl.semaphore_wait(barrier, 23)
+    for dz in PLANES:
+        pl.semaphore_signal(
+            plane_sem.at[z], inc=1, device_id=(((z + dz) & 7) * 2 + core, seq), device_id_type=MESH
+        )
     far_lanes = pl.ds(pl.multiple_of(other * 256, 256), 256)
     near_lanes = pl.multiple_of(core * 256, 256)
     swaps = [
@@ -118,8 +124,6 @@
     ]
     for swap in swaps:
         swap.start()
-    for dz in in_line:
-        pl.semaphore_signal(round_sem, inc=1, device_id=(((z + dz) & 7) * 2 + core, seq), device_id_type=MESH)
 
     def place(block, ab, start):
         send[pl.ds(ab * 1024 + start, CHIPS, stride=8), :] = block.T
@@ -137,8 +141,8 @@
             rows, lanes = pl.ds(half * 128, 128), pl.ds(ab * 128, 128)
             place(source[rows, lanes], ab, at + 2 * other + half)
 
-    def spread(source, target, base, size, sends, receives):
-        for dz, dx, dy in FAR_FIRST:
+    def spread(source, target, base, size, sends, receives, offsets=FAR_FIRST):
+        for dz, dx, dy in offsets:
             to_z = (z + dz) & 7
             to_seq = ((seq + 4 * dx) & 12) | ((seq + dy) & 3)
             to_chip = to_z * 16 + to_seq
@@ -153,8 +157,10 @@
         slabs = buffer.at[pl.ds(0, (CHIPS - 1) * size)]
         pltpu.make_async_copy(slabs, slabs, semaphore).wait()
 
-    def send_slabs(ab):
-        spread(send, recv, ab * 1024, 8, send_sem.at[ab], recv_sem.at[ab])
+    def send_slabs(ab, offsets):
+        spread(send, recv, ab * 1024, 8, send_sem.at[ab], recv_sem.at[ab], offsets)
+
+    def keep_slab(ab):
         own = pl.ds(pl.multiple_of(ab * 1024 + chip * 8, 8), 8)
         recv[own, :] = send[own, :]
 
@@ -163,11 +169,15 @@
     for which in range(2):
         swaps[which].wait_recv()
         place_sibling(0, which)
-    pl.semaphore_wait(round_sem, 7)
-    send_slabs(0)
+    send_slabs(0, [offset for offset in FAR_FIRST if offset[0] == 0])
+    for dz in PLANES:
+        pl.semaphore_wait(plane_sem.at[(z + dz) & 7], 1)
+        send_slabs(0, [offset for offset in FAR_FIRST if offset[0] == dz])
     for which in range(2):
         place_sibling(1, which)
-    send_slabs(1)
+    send_slabs(1, FAR_FIRST)
+    keep_slab(0)
+    keep_slab(1)
 
     for load in loads[2:]:
         load.wait()
@@ -299,7 +309,7 @@
         v((512, 512), F32), v((512, 1024), BF16), v((512, 512), F32), v((256, 1024), BF16), v((256, 512), F32),
         v((1536, 256), BF16), v((2, 256, 256), F32), v((2, 128, 256), F32), v((1024, 128), F32), v((1024, 128), F32),
         pltpu.SemaphoreType.DMA((9,)), pltpu.SemaphoreType.DMA((4,)), pltpu.SemaphoreType.DMA((4,)),
-        pltpu.SemaphoreType.DMA((4,)), pltpu.SemaphoreType.DMA((4,)), pltpu.SemaphoreType.REGULAR,
+        pltpu.SemaphoreType.DMA((4,)), pltpu.SemaphoreType.DMA((4,)), pltpu.SemaphoreType.REGULAR((8,)),
     ]
     operands = [pltpu.with_memory_space_constraint(x, pltpu.HBM) for x in (signal, gating, kernel, bypass, *consts)]
     return pl.pallas_call(

time: 54 us -> 54.8 us (1.015)
  Pallas kernels: 53.2 us -> 54 us
    pallas_call x1, Pallas kernels: 53.2 us -> 54 us  [on_device(): pl.pallas_call(kernel_body, out_shape=pltpu.VMEM((256, 512), BF16), in_sp...]
where the time goes in v5:
time: 54.8 us
  Pallas kernels  54 us (99%)
  local copies, waits for them, and re-layouts  0.71 us (1%)
    pallas_call x1, Pallas kernels, on_device(): pl.pallas_call(kernel_body, out_shape=pltpu.VMEM((256, 512), BF16), in_sp...  54 us

profile of v5, /device:TPU:1, one launch (start us, length us, event | category | flops | bytes accessed | tf_op | source)
XLA Modules:
  0.0 54.8 jit_solution(9102669789249296194)
XLA Ops:
  0.0 54.0 %hyena.1 = bf16[256,512]{1,0:T(8,128)(2,1)S(1)} custom-call(bf16[256,512]{1,0:T(8,128)(2,1)} %sig_hbm.1, bf16[256,512]{1,0:T(8,128)(2,1)} %gate_hbm.1, f32[256,512]{1,0:T(8,128)} %ker_hbm.1, f32[512]{0:T(512)} %byp_hbm.1, bf16[512,768]{1,0:T(8,128)(2,1)} %constant.10.clone.first_hbm, f32[256,512]{1,0:T(8,128)} %constant.11.clone.turn_hbm, ...), custom_call_target="tpu_custom_call" | custom-call | tf_op jit(solution)/shard_map/hyena/pallas_call | solution.py:315
  54.1 0.7 %copy.11 = bf16[256,512]{1,0:T(8,128)(2,1)} copy(bf16[256,512]{1,0:T(8,128)(2,1)S(1)} %hyena.1) | data formatting | bytes 524288

commit v6 on v4

--- a/solution.py
+++ b/solution.py
@@ -72,8 +72,8 @@
     sig_hbm, gate_hbm, ker_hbm, byp_hbm, first_hbm, turn_hbm, fwd_hbm, bwd_hbm, last_hbm,
     out_ref,
     sig, gate, ker, byp, first, turn, fwd, bwd, last,
-    wide, sib_u, sib_k, send, recv, a_buf, b_buf, x_buf, p_buf, c_buf, d_buf, y_buf, y_sib, y_send, y_recv,
-    load_sem, sib_send, sib_recv, send_sem, recv_sem, round_sem,
+    wide, sib_u, sib_k, post_out, post_in, send, recv, u_mat, k_mat, a_buf, b_buf, x_buf, p_buf, c_buf, d_buf, y_buf, y_sib, y_send, y_recv,
+    load_sem, sib_send, sib_recv, send_sem, recv_sem, in_sem,
 ):
     grp, seq = lax.axis_index("grp"), lax.axis_index("seq")
     z, core = grp // 2, grp % 2
@@ -82,14 +82,14 @@
     sibling = (z * 2 + other, seq)
 
     barrier = pltpu.get_barrier_semaphore()
-    in_line = (4, 3, 5, 2, 6, 1, 7)
-    for dz in in_line:
-        pl.semaphore_signal(barrier, inc=1, device_id=(((z + dz) & 7) * 2 + core, seq), device_id_type=MESH)
+
+    @pl.when(core == 1)
+    def _():
+        pl.semaphore_signal(barrier, inc=1, device_id=sibling, device_id_type=MESH)
+
     for dz, dx, dy in FAR_FIRST:
-        if dz == 0:
-            mate = ((seq + 4 * dx) & 12) | ((seq + dy) & 3)
-            pl.semaphore_signal(barrier, inc=1, device_id=(grp, mate), device_id_type=MESH)
-    pl.semaphore_signal(barrier, inc=1, device_id=sibling, device_id_type=MESH)
+        mate = (((z + dz) & 7) * 2 + core, ((seq + 4 * dx) & 12) | ((seq + dy) & 3))
+        pl.semaphore_signal(barrier, inc=1, device_id=mate, device_id_type=MESH)
 
     loads = [
         pltpu.make_async_copy(source, target, load_sem.at[i])
@@ -105,40 +105,33 @@
     loads[0].wait()
     loads[1].wait()
     wide[...] = sig[...].astype(F32)
-
-    pl.semaphore_wait(barrier, 23)
-    far_lanes = pl.ds(pl.multiple_of(other * 256, 256), 256)
-    near_lanes = pl.multiple_of(core * 256, 256)
-    swaps = [
-        pltpu.make_async_remote_copy(
-            src_ref=source.at[:, far_lanes], dst_ref=target, send_sem=sib_send.at[i], recv_sem=sib_recv.at[i],
-            device_id=sibling, device_id_type=MESH,
-        )
-        for i, (source, target) in enumerate([(ker, sib_k), (wide, sib_u)])
-    ]
-    for swap in swaps:
-        swap.start()
-    for dz in in_line:
-        pl.semaphore_signal(round_sem, inc=1, device_id=(((z + dz) & 7) * 2 + core, seq), device_id_type=MESH)
+    near_lanes = pl.multiple_of(core * 256 + 128, 128)
+    far_lanes = pl.multiple_of(other * 256 + 128, 128)
 
     def place(block, ab, start):
         send[pl.ds(ab * 1024 + start, CHIPS, stride=8), :] = block.T
 
-    def place_near(ab):
+    for half in range(2):
+        rows = slice(half * 128, half * 128 + 128)
+        for owner in range(2):
+            lanes = slice(owner * 256, owner * 256 + 128)
+            place(wide[rows, lanes], 0, 2 * owner + half)
+            place(ker[rows, lanes], 0, 4 + 2 * owner + half)
+
+    def place_near():
         for half in range(2):
-            rows = pl.ds(half * 128, 128)
-            lanes = pl.ds(near_lanes + ab * 128, 128)
-            place(ker[rows, lanes], ab, 4 + 2 * core + half)
-            place(wide[rows, lanes], ab, 2 * core + half)
-
-    def place_sibling(ab, which):
-        source, at = ((sib_k, 4), (sib_u, 0))[which]
+            rows = slice(half * 128, half * 128 + 128)
+            place(wide[rows, pl.ds(near_lanes, 128)], 1, 2 * core + half)
+            place(ker[rows, pl.ds(near_lanes, 128)], 1, 4 + 2 * core + half)
+
+    def place_sibling():
         for half in range(2):
-            rows, lanes = pl.ds(half * 128, 128), pl.ds(ab * 128, 128)
-            place(source[rows, lanes], ab, at + 2 * other + half)
-
-    def spread(source, target, base, size, sends, receives):
-        for dz, dx, dy in FAR_FIRST:
+            rows = slice(half * 128, half * 128 + 128)
+            place(sib_u[rows, :], 1, 2 * other + half)
+            place(sib_k[rows, :], 1, 4 + 2 * other + half)
+
+    def spread(source, target, base, size, sends, receives, offsets=FAR_FIRST):
+        for dz, dx, dy in offsets:
             to_z = (z + dz) & 7
             to_seq = ((seq + 4 * dx) & 12) | ((seq + dy) & 3)
             to_chip = to_z * 16 + to_seq
@@ -153,21 +146,39 @@
         slabs = buffer.at[pl.ds(0, (CHIPS - 1) * size)]
         pltpu.make_async_copy(slabs, slabs, semaphore).wait()
 
-    def send_slabs(ab):
-        spread(send, recv, ab * 1024, 8, send_sem.at[ab], recv_sem.at[ab])
+    def send_slabs(ab, offsets):
+        spread(send, recv, ab * 1024, 8, send_sem.at[ab], recv_sem.at[ab], offsets)
+
+    pl.semaphore_wait(barrier, CHIPS - core)
+
+    @pl.when(core == 0)
+    def _():
+        pl.semaphore_signal(in_sem, inc=1, device_id=sibling, device_id_type=MESH)
+
+    send_slabs(0, FAR_FIRST[:64])
+
+    @pl.when(core == 1)
+    def _():
+        pl.semaphore_wait(in_sem, 1)
+
+    swaps = [
+        pltpu.make_async_remote_copy(
+            src_ref=source.at[:, pl.ds(far_lanes, 128)], dst_ref=target, send_sem=sib_send.at[i],
+            recv_sem=sib_recv.at[i], device_id=sibling, device_id_type=MESH,
+        )
+        for i, (source, target) in enumerate([(ker, sib_k), (wide, sib_u)])
+    ]
+    for swap in swaps:
+        swap.start()
+    send_slabs(0, FAR_FIRST[64:])
+    place_near()
+    for swap in swaps:
+        swap.wait_recv()
+    place_sibling()
+    send_slabs(1, FAR_FIRST)
+    for ab in range(2):
         own = pl.ds(pl.multiple_of(ab * 1024 + chip * 8, 8), 8)
         recv[own, :] = send[own, :]
-
-    place_near(0)
-    place_near(1)
-    for which in range(2):
-        swaps[which].wait_recv()
-        place_sibling(0, which)
-    pl.semaphore_wait(round_sem, 7)
-    send_slabs(0)
-    for which in range(2):
-        place_sibling(1, which)
-    send_slabs(1)
 
     for load in loads[2:]:
         load.wait()
@@ -178,19 +189,47 @@
             send_sem=sib_send.at[2 + ab], recv_sem=sib_recv.at[2 + ab], device_id=sibling, device_id_type=MESH,
         )
 
+    post_swap = pltpu.make_async_remote_copy(
+        src_ref=post_out, dst_ref=post_in, send_sem=sib_send.at[4], recv_sem=sib_recv.at[4],
+        device_id=sibling, device_id_type=MESH,
+    )
+
     @pl.loop(0, 2)
     def _(ab):
         drain(recv, 8, recv_sem.at[ab])
-        base = pl.multiple_of(ab * 1024, 1024)
-
-        def rows_of(t):
-            top = [recv[pl.ds(base + t + half, CHIPS, stride=8), :] for half in range(2)]
-            low = [recv[pl.ds(base + t + 2 + half, CHIPS, stride=8), :] for half in range(2)]
-            return jnp.concatenate([jnp.concatenate(top, axis=1), jnp.concatenate(low, axis=1)], axis=0)
-
-        u = rows_of(0).astype(BF16)
+
+        def arrived(t):
+            return recv[pl.ds(ab * 1024 + t, CHIPS, stride=8), :]
+
+        def keep(which, half, u, k):
+            rows = pl.ds(pl.multiple_of(which * 128, 128), 128)
+            low_rows = pl.ds(pl.multiple_of(256 + which * 128, 128), 128)
+            lanes = slice(half * 128, half * 128 + 128)
+            u_mat[rows, lanes] = u.astype(BF16)
+            k_mat[rows, lanes], k_mat[low_rows, lanes] = halves(k)
+
+        @pl.when(ab == 0)
+        def _():
+            for half in range(2):
+                post_out[half * 128 : half * 128 + 128, :] = arrived(2 * other + half)
+                post_out[256 + half * 128 : 384 + half * 128, :] = arrived(4 + 2 * other + half)
+            post_swap.start()
+            for half in range(2):
+                keep(core, half, arrived(2 * core + half), arrived(4 + 2 * core + half))
+            post_swap.wait_recv()
+            for half in range(2):
+                from_sibling = slice(half * 128, half * 128 + 128), slice(256 + half * 128, 384 + half * 128)
+                keep(other, half, post_in[from_sibling[0], :], post_in[from_sibling[1], :])
+
+        @pl.when(ab == 1)
+        def _():
+            for which in range(2):
+                for half in range(2):
+                    keep(which, half, arrived(2 * which + half), arrived(4 + 2 * which + half))
+
+        u = u_mat[...]
         u_twice = jnp.concatenate([u, u], axis=0)
-        k_high, k_low = halves(rows_of(4))
+        k_high, k_low = k_mat[0:256, :], k_mat[256:512, :]
         k_thrice = jnp.concatenate([k_high, k_high, k_low], axis=0)
 
         def columns(part):
@@ -254,8 +293,7 @@
         factor = byp[core * 256 + ab * CHIPS + chip]
 
         def u_part(which):
-            part = [recv[pl.ds(base + 2 * which + half, CHIPS, stride=8), :] for half in range(2)]
-            return jnp.concatenate(part, axis=1)
+            return u_mat[pl.ds(pl.multiple_of(which * 128, 128), 128), :].astype(F32)
 
         near = pl.ds(pl.multiple_of(core * 128, 128), 128)
         away = pl.ds(pl.multiple_of(other * 128, 128), 128)
@@ -281,6 +319,7 @@
             at = (slice(half, half + 128), slice(ch, ch + 128))
             out_ref[at] = (mixed * gate[at].astype(F32)).astype(BF16)
 
+    post_swap.wait_send()
     for ab in range(2):
         swaps[ab].wait_send()
         y_swap(ab).wait_send()
@@ -294,11 +333,11 @@
     scratch = [
         v((256, 512), BF16), v((256, 512), BF16), v((256, 512), F32), pltpu.SMEM((512,), F32),
         *[v(c.shape, c.dtype) for c in consts],
-        v((256, 512), F32), v((256, 256), F32), v((256, 256), F32),
-        v((2048, 128), F32), v((2048, 128), F32),
+        v((256, 512), F32), v((256, 128), F32), v((256, 128), F32), v((512, 128), F32), v((512, 128), F32),
+        v((2048, 128), F32), v((2048, 128), F32), v((256, 256), BF16), v((512, 256), BF16),
         v((512, 512), F32), v((512, 1024), BF16), v((512, 512), F32), v((256, 1024), BF16), v((256, 512), F32),
         v((1536, 256), BF16), v((2, 256, 256), F32), v((2, 128, 256), F32), v((1024, 128), F32), v((1024, 128), F32),
-        pltpu.SemaphoreType.DMA((9,)), pltpu.SemaphoreType.DMA((4,)), pltpu.SemaphoreType.DMA((4,)),
+        pltpu.SemaphoreType.DMA((9,)), pltpu.SemaphoreType.DMA((5,)), pltpu.SemaphoreType.DMA((5,)),
         pltpu.SemaphoreType.DMA((4,)), pltpu.SemaphoreType.DMA((4,)), pltpu.SemaphoreType.REGULAR,
     ]
     operands = [pltpu.with_memory_space_constraint(x, pltpu.HBM) for x in (signal, gating, kernel, bypass, *consts)]

time: 54 us -> 53.6 us (level)
  no operation moved by 1% of the time
where the time goes in v6:
time: 53.6 us; the launch traced here: 53.5 us
  Pallas kernels  52.8 us (99%)
  local copies, waits for them, and re-layouts  0.71 us (1%)
    pallas_call x1, Pallas kernels, on_device(): pl.pallas_call(kernel_body, out_shape=pltpu.VMEM((256, 512), BF16), in_sp...  52.8 us

profile of v6, /device:TPU:1, one launch (start us, length us, event | category | flops | bytes accessed | tf_op | source)
XLA Modules:
  0.0 53.5 jit_solution(17029860316201874957)
XLA Ops:
  0.0 52.8 %hyena.1 = bf16[256,512]{1,0:T(8,128)(2,1)S(1)} custom-call(bf16[256,512]{1,0:T(8,128)(2,1)} %sig_hbm.1, bf16[256,512]{1,0:T(8,128)(2,1)} %gate_hbm.1, f32[256,512]{1,0:T(8,128)} %ker_hbm.1, f32[512]{0:T(512)} %byp_hbm.1, bf16[512,768]{1,0:T(8,128)(2,1)} %constant.10.clone.first_hbm, f32[256,512]{1,0:T(8,128)} %constant.11.clone.turn_hbm, ...), custom_call_target="tpu_custom_call" | custom-call | tf_op jit(solution)/shard_map/hyena/pallas_call | solution.py:344
  52.8 0.7 %copy.11 = bf16[256,512]{1,0:T(8,128)(2,1)} copy(bf16[256,512]{1,0:T(8,128)(2,1)S(1)} %hyena.1) | data formatting | bytes 524288

commit v7 on v6

--- a/solution.py
+++ b/solution.py
@@ -81,16 +81,6 @@
     chip = z * 16 + seq
     sibling = (z * 2 + other, seq)
 
-    barrier = pltpu.get_barrier_semaphore()
-
-    @pl.when(core == 1)
-    def _():
-        pl.semaphore_signal(barrier, inc=1, device_id=sibling, device_id_type=MESH)
-
-    for dz, dx, dy in FAR_FIRST:
-        mate = (((z + dz) & 7) * 2 + core, ((seq + 4 * dx) & 12) | ((seq + dy) & 3))
-        pl.semaphore_signal(barrier, inc=1, device_id=mate, device_id_type=MESH)
-
     loads = [
         pltpu.make_async_copy(source, target, load_sem.at[i])
         for i, (source, target) in enumerate(
@@ -100,8 +90,18 @@
             ]
         )
     ]
-    for load in loads:
+    for load in loads[:2]:
         load.start()
+    barrier = pltpu.get_barrier_semaphore()
+
+    @pl.when(core == 1)
+    def _():
+        pl.semaphore_signal(barrier, inc=1, device_id=sibling, device_id_type=MESH)
+
+    for dz, dx, dy in FAR_FIRST:
+        mate = (((z + dz) & 7) * 2 + core, ((seq + 4 * dx) & 12) | ((seq + dy) & 3))
+        pl.semaphore_signal(barrier, inc=1, device_id=mate, device_id_type=MESH)
+
     loads[0].wait()
     loads[1].wait()
     wide[...] = sig[...].astype(F32)
@@ -156,6 +156,8 @@
         pl.semaphore_signal(in_sem, inc=1, device_id=sibling, device_id_type=MESH)
 
     send_slabs(0, FAR_FIRST[:64])
+    for load in loads[2:]:
+        load.start()
 
     @pl.when(core == 1)
     def _():

time: 53.6 us -> 53.6 us (level)
  no operation moved by 1% of the time
where the time goes in v7:
time: 53.6 us; the launch traced here: 53.5 us
  Pallas kernels  52.8 us (99%)
  local copies, waits for them, and re-layouts  0.71 us (1%)
    pallas_call x1, Pallas kernels, on_device(): pl.pallas_call(kernel_body, out_shape=pltpu.VMEM((256, 512), BF16), in_sp...  52.8 us

profile of v7, /device:TPU:1, one launch (start us, length us, event | category | flops | bytes accessed | tf_op | source)
XLA Modules:
  0.0 53.5 jit_solution(14831258748207131453)
XLA Ops:
  0.0 52.8 %hyena.1 = bf16[256,512]{1,0:T(8,128)(2,1)S(1)} custom-call(bf16[256,512]{1,0:T(8,128)(2,1)} %sig_hbm.1, bf16[256,512]{1,0:T(8,128)(2,1)} %gate_hbm.1, f32[256,512]{1,0:T(8,128)} %ker_hbm.1, f32[512]{0:T(512)} %byp_hbm.1, bf16[512,768]{1,0:T(8,128)(2,1)} %constant.10.clone.first_hbm, f32[256,512]{1,0:T(8,128)} %constant.11.clone.turn_hbm, ...), custom_call_target="tpu_custom_call" | custom-call | tf_op jit(solution)/shard_map/hyena/pallas_call | solution.py:346
  52.8 0.7 %copy.11 = bf16[256,512]{1,0:T(8,128)(2,1)} copy(bf16[256,512]{1,0:T(8,128)(2,1)S(1)} %hyena.1) | data formatting | bytes 524288

commit v8 on v7

--- a/solution.py
+++ b/solution.py
@@ -72,7 +72,7 @@
     sig_hbm, gate_hbm, ker_hbm, byp_hbm, first_hbm, turn_hbm, fwd_hbm, bwd_hbm, last_hbm,
     out_ref,
     sig, gate, ker, byp, first, turn, fwd, bwd, last,
-    wide, sib_u, sib_k, post_out, post_in, send, recv, u_mat, k_mat, a_buf, b_buf, x_buf, p_buf, c_buf, d_buf, y_buf, y_sib, y_send, y_recv,
+    wide, sib_u, sib_k, post_out, post_in, send, recv, u_mat, k_mat, a_buf, b_buf, x_buf, p_buf, c_buf, d_buf, y_buf, y_out, y_in, y_send, y_recv,
     load_sem, sib_send, sib_recv, send_sem, recv_sem, in_sem,
 ):
     grp, seq = lax.axis_index("grp"), lax.axis_index("seq")
@@ -187,7 +187,7 @@
 
     def y_swap(ab):
         return pltpu.make_async_remote_copy(
-            src_ref=y_buf.at[ab, pl.ds(pl.multiple_of(other * 128, 128), 128)], dst_ref=y_sib.at[ab],
+            src_ref=y_out.at[ab], dst_ref=y_in.at[ab],
             send_sem=sib_send.at[2 + ab], recv_sem=sib_recv.at[2 + ab], device_id=sibling, device_id_type=MESH,
         )
 
@@ -294,32 +294,32 @@
 
         factor = byp[core * 256 + ab * CHIPS + chip]
 
-        def u_part(which):
-            return u_mat[pl.ds(pl.multiple_of(which * 128, 128), 128), :].astype(F32)
-
-        near = pl.ds(pl.multiple_of(core * 128, 128), 128)
-        away = pl.ds(pl.multiple_of(other * 128, 128), 128)
-        y_buf[ab, away] = dot(last[away, :], d_buf[...]) + factor * u_part(other)
-        swap = y_swap(ab)
-        swap.start()
-        y_buf[ab, near] = dot(last[near, :], d_buf[...]) + factor * u_part(core)
+        direct = factor * u_mat[...].astype(F32)
+        y_buf[...] = dot(last[...], d_buf[...]) + direct
         at = pl.multiple_of(ab * 512, 512)
-        for half in range(2):
-            y_send[pl.ds(at + 2 * core + half, CHIPS, stride=4), :] = y_buf[ab, near, half * 128 : half * 128 + 128]
-        swap.wait_recv()
-        for half in range(2):
-            y_send[pl.ds(at + 2 * other + half, CHIPS, stride=4), :] = y_sib[ab, :, half * 128 : half * 128 + 128]
+        for t in range(4):
+            which, half = t // 2 * 128, t % 2 * 128
+            y_send[pl.ds(at + t, CHIPS, stride=4), :] = y_buf[which : which + 128, half : half + 128]
         spread(y_send, y_recv, at, 4, send_sem.at[2 + ab], recv_sem.at[2 + ab])
         own = pl.ds(pl.multiple_of(at + chip * 4, 4), 4)
         y_recv[own, :] = y_send[own, :]
 
+    def finish(owner, ab, half, values):
+        rows, lanes = slice(half * 128, half * 128 + 128), pl.ds(pl.multiple_of(owner * 256 + ab * 128, 128), 128)
+        out_ref[rows, lanes] = (values.T * gate[rows, lanes].astype(F32)).astype(BF16)
+
     for ab in range(2):
         drain(y_recv, 4, recv_sem.at[2 + ab])
-        for t in range(4):
-            ch, half = t // 2 * 256 + ab * 128, t % 2 * 128
-            mixed = y_recv[pl.ds(ab * 512 + t, CHIPS, stride=4), :].T
-            at = (slice(half, half + 128), slice(ch, ch + 128))
-            out_ref[at] = (mixed * gate[at].astype(F32)).astype(BF16)
+        for half in range(2):
+            y_out[ab, half * 128 : half * 128 + 128, :] = y_recv[
+                pl.ds(ab * 512 + 2 * other + half, CHIPS, stride=4), :
+            ]
+        y_swap(ab).start()
+        for half in range(2):
+            finish(core, ab, half, y_recv[pl.ds(ab * 512 + 2 * core + half, CHIPS, stride=4), :])
+        y_swap(ab).wait_recv()
+        for half in range(2):
+            finish(other, ab, half, y_in[ab, half * 128 : half * 128 + 128, :])
 
     post_swap.wait_send()
     for ab in range(2):
@@ -338,7 +338,7 @@
         v((256, 512), F32), v((256, 128), F32), v((256, 128), F32), v((512, 128), F32), v((512, 128), F32),
         v((2048, 128), F32), v((2048, 128), F32), v((256, 256), BF16), v((512, 256), BF16),
         v((512, 512), F32), v((512, 1024), BF16), v((512, 512), F32), v((256, 1024), BF16), v((256, 512), F32),
-        v((1536, 256), BF16), v((2, 256, 256), F32), v((2, 128, 256), F32), v((1024, 128), F32), v((1024, 128), F32),
+        v((1536, 256), BF16), v((256, 256), F32), v((2, 256, 128), F32), v((2, 256, 128), F32), v((1024, 128), F32), v((1024, 128), F32),
         pltpu.SemaphoreType.DMA((9,)), pltpu.SemaphoreType.DMA((5,)), pltpu.SemaphoreType.DMA((5,)),
         pltpu.SemaphoreType.DMA((4,)), pltpu.SemaphoreType.DMA((4,)), pltpu.SemaphoreType.REGULAR,
     ]

time: 53.6 us -> 52.7 us (0.983)
  Pallas kernels: 52.8 us -> 51.9 us
    pallas_call x1, Pallas kernels: 52.8 us -> 51.9 us  [on_device(): pl.pallas_call(kernel_body, out_shape=pltpu.VMEM((256, 512), BF16), in_sp...]
where the time goes in v8:
time: 52.7 us
  Pallas kernels  51.9 us (98%)
  local copies, waits for them, and re-layouts  0.71 us (1%)
    pallas_call x1, Pallas kernels, on_device(): pl.pallas_call(kernel_body, out_shape=pltpu.VMEM((256, 512), BF16), in_sp...  51.9 us

profile of v8, /device:TPU:1, one launch (start us, length us, event | category | flops | bytes accessed | tf_op | source)
XLA Modules:
  0.0 52.7 jit_solution(5300885235634882621)
XLA Ops:
  0.0 51.9 %hyena.1 = bf16[256,512]{1,0:T(8,128)(2,1)S(1)} custom-call(bf16[256,512]{1,0:T(8,128)(2,1)} %sig_hbm.1, bf16[256,512]{1,0:T(8,128)(2,1)} %gate_hbm.1, f32[256,512]{1,0:T(8,128)} %ker_hbm.1, f32[512]{0:T(512)} %byp_hbm.1, bf16[512,768]{1,0:T(8,128)(2,1)} %constant.10.clone.first_hbm, f32[256,512]{1,0:T(8,128)} %constant.11.clone.turn_hbm, ...), custom_call_target="tpu_custom_call" | custom-call | tf_op jit(solution)/shard_map/hyena/pallas_call | solution.py:346
  51.9 0.7 %copy.11 = bf16[256,512]{1,0:T(8,128)(2,1)} copy(bf16[256,512]{1,0:T(8,128)(2,1)S(1)} %hyena.1) | data formatting | bytes 524288

commit v9 on v8

--- a/solution.py
+++ b/solution.py
@@ -78,6 +78,7 @@
     grp, seq = lax.axis_index("grp"), lax.axis_index("seq")
     z, core = grp // 2, grp % 2
     other = 1 - core
+    way = 1 - 2 * core
     chip = z * 16 + seq
     sibling = (z * 2 + other, seq)
 
@@ -132,8 +133,8 @@
 
     def spread(source, target, base, size, sends, receives, offsets=FAR_FIRST):
         for dz, dx, dy in offsets:
-            to_z = (z + dz) & 7
-            to_seq = ((seq + 4 * dx) & 12) | ((seq + dy) & 3)
+            to_z = (z + way * dz) & 7
+            to_seq = ((seq + 4 * way * dx) & 12) | ((seq + way * dy) & 3)
             to_chip = to_z * 16 + to_seq
             pltpu.make_async_remote_copy(
                 src_ref=source.at[pl.ds(pl.multiple_of(base + to_chip * size, size), size)],

time: 52.7 us -> 52.5 us (level)
  no operation moved by 1% of the time
where the time goes in v9:
time: 52.5 us; the launch traced here: 52.4 us
  Pallas kernels  51.7 us (98%)
  local copies, waits for them, and re-layouts  0.71 us (1%)
    pallas_call x1, Pallas kernels, on_device(): pl.pallas_call(kernel_body, out_shape=pltpu.VMEM((256, 512), BF16), in_sp...  51.7 us

profile of v9, /device:TPU:1, one launch (start us, length us, event | category | flops | bytes accessed | tf_op | source)
XLA Modules:
  0.0 52.4 jit_solution(2010460089224310517)
XLA Ops:
  0.0 51.7 %hyena.1 = bf16[256,512]{1,0:T(8,128)(2,1)S(1)} custom-call(bf16[256,512]{1,0:T(8,128)(2,1)} %sig_hbm.1, bf16[256,512]{1,0:T(8,128)(2,1)} %gate_hbm.1, f32[256,512]{1,0:T(8,128)} %ker_hbm.1, f32[512]{0:T(512)} %byp_hbm.1, bf16[512,768]{1,0:T(8,128)(2,1)} %constant.10.clone.first_hbm, f32[256,512]{1,0:T(8,128)} %constant.11.clone.turn_hbm, ...), custom_call_target="tpu_custom_call" | custom-call | tf_op jit(solution)/shard_map/hyena/pallas_call | solution.py:347
  51.7 0.7 %copy.11 = bf16[256,512]{1,0:T(8,128)(2,1)} copy(bf16[256,512]{1,0:T(8,128)(2,1)S(1)} %hyena.1) | data formatting | bytes 524288

commit v10 on v9

--- a/solution.py
+++ b/solution.py
@@ -337,9 +337,9 @@
         v((256, 512), BF16), v((256, 512), BF16), v((256, 512), F32), pltpu.SMEM((512,), F32),
         *[v(c.shape, c.dtype) for c in consts],
         v((256, 512), F32), v((256, 128), F32), v((256, 128), F32), v((512, 128), F32), v((512, 128), F32),
-        v((2048, 128), F32), v((2048, 128), F32), v((256, 256), BF16), v((512, 256), BF16),
+        v((2056, 128), F32), v((2056, 128), F32), v((256, 256), BF16), v((512, 256), BF16),
         v((512, 512), F32), v((512, 1024), BF16), v((512, 512), F32), v((256, 1024), BF16), v((256, 512), F32),
-        v((1536, 256), BF16), v((256, 256), F32), v((2, 256, 128), F32), v((2, 256, 128), F32), v((1024, 128), F32), v((1024, 128), F32),
+        v((1536, 256), BF16), v((256, 256), F32), v((2, 256, 128), F32), v((2, 256, 128), F32), v((1032, 128), F32), v((1032, 128), F32),
         pltpu.SemaphoreType.DMA((9,)), pltpu.SemaphoreType.DMA((5,)), pltpu.SemaphoreType.DMA((5,)),
         pltpu.SemaphoreType.DMA((4,)), pltpu.SemaphoreType.DMA((4,)), pltpu.SemaphoreType.REGULAR,
     ]

time: 52.5 us -> 52.5 us (level)
  no operation moved by 1% of the time
where the time goes in v10:
time: 52.5 us; the launch traced here: 52.4 us
  Pallas kernels  51.7 us (98%)
  local copies, waits for them, and re-layouts  0.71 us (1%)
    pallas_call x1, Pallas kernels, on_device(): pl.pallas_call(kernel_body, out_shape=pltpu.VMEM((256, 512), BF16), in_sp...  51.7 us

profile of v10, /device:TPU:1, one launch (start us, length us, event | category | flops | bytes accessed | tf_op | source)
XLA Modules:
  0.0 52.4 jit_solution(3651846294492928145)
XLA Ops:
  0.0 51.7 %hyena.1 = bf16[256,512]{1,0:T(8,128)(2,1)S(1)} custom-call(bf16[256,512]{1,0:T(8,128)(2,1)} %sig_hbm.1, bf16[256,512]{1,0:T(8,128)(2,1)} %gate_hbm.1, f32[256,512]{1,0:T(8,128)} %ker_hbm.1, f32[512]{0:T(512)} %byp_hbm.1, bf16[512,768]{1,0:T(8,128)(2,1)} %constant.10.clone.first_hbm, f32[256,512]{1,0:T(8,128)} %constant.11.clone.turn_hbm, ...), custom_call_target="tpu_custom_call" | custom-call | tf_op jit(solution)/shard_map/hyena/pallas_call | solution.py:347
  51.7 0.7 %copy.11 = bf16[256,512]{1,0:T(8,128)(2,1)} copy(bf16[256,512]{1,0:T(8,128)(2,1)S(1)} %hyena.1) | data formatting | bytes 524288

commit v11 on v10

--- a/solution.py
+++ b/solution.py
@@ -281,16 +281,16 @@
                     d_buf[1024 + at : 1056 + at, :] = low
 
         columns(0)
+        twist(0)
         columns(1)
-        twist(0)
         x_buf[0:256, :] = three(b_buf, fwd, slice(0, 256))
         twist(1)
         x_buf[256:512, :] = three(b_buf, fwd, slice(256, 512))
         product(0)
         c_buf[0:128, :] = three(p_buf, bwd, slice(0, 128))
         product(1)
+        untwist(0)
         c_buf[128:256, :] = three(p_buf, bwd, slice(128, 256))
-        untwist(0)
         untwist(1)
 
         factor = byp[core * 256 + ab * CHIPS + chip]

time: 52.5 us -> 52.5 us (level)
  no operation moved by 1% of the time
where the time goes in v11:
time: 52.5 us; the launch traced here: 52.4 us
  Pallas kernels  51.7 us (98%)
  local copies, waits for them, and re-layouts  0.71 us (1%)
    pallas_call x1, Pallas kernels, on_device(): pl.pallas_call(kernel_body, out_shape=pltpu.VMEM((256, 512), BF16), in_sp...  51.7 us

profile of v11, /device:TPU:1, one launch (start us, length us, event | category | flops | bytes accessed | tf_op | source)
XLA Modules:
  0.0 52.4 jit_solution(3651846294492928145)
XLA Ops:
  0.0 51.7 %hyena.1 = bf16[256,512]{1,0:T(8,128)(2,1)S(1)} custom-call(bf16[256,512]{1,0:T(8,128)(2,1)} %sig_hbm.1, bf16[256,512]{1,0:T(8,128)(2,1)} %gate_hbm.1, f32[256,512]{1,0:T(8,128)} %ker_hbm.1, f32[512]{0:T(512)} %byp_hbm.1, bf16[512,768]{1,0:T(8,128)(2,1)} %constant.10.clone.first_hbm, f32[256,512]{1,0:T(8,128)} %constant.11.clone.turn_hbm, ...), custom_call_target="tpu_custom_call" | custom-call | tf_op jit(solution)/shard_map/hyena/pallas_call | solution.py:347
  51.7 0.7 %copy.11 = bf16[256,512]{1,0:T(8,128)(2,1)} copy(bf16[256,512]{1,0:T(8,128)(2,1)S(1)} %hyena.1) | data formatting | bytes 524288

commit v12 on v10

--- a/solution.py
+++ b/solution.py
@@ -24,6 +24,17 @@
 
 OFFSETS = [(dz, dx, dy) for dx in range(4) for dy in range(4) for dz in range(8)]
 FAR_FIRST = sorted(OFFSETS[1:], key=lambda offset: -hops(offset))
+
+
+def alternate(offsets):
+    turns = [[], [], []]
+    for offset in offsets:
+        turns[0 if 0 < offset[0] < 4 else 1 if offset[0] > 4 else 2].append(offset)
+    longest = max(len(turn) for turn in turns)
+    return [turn[i] for i in range(longest) for turn in turns if i < len(turn)]
+
+
+ALTERNATE = alternate(FAR_FIRST)
 
 
 def split_table(table):
@@ -301,7 +312,7 @@
         for t in range(4):
             which, half = t // 2 * 128, t % 2 * 128
             y_send[pl.ds(at + t, CHIPS, stride=4), :] = y_buf[which : which + 128, half : half + 128]
-        spread(y_send, y_recv, at, 4, send_sem.at[2 + ab], recv_sem.at[2 + ab])
+        spread(y_send, y_recv, at, 4, send_sem.at[2 + ab], recv_sem.at[2 + ab], ALTERNATE)
         own = pl.ds(pl.multiple_of(at + chip * 4, 4), 4)
         y_recv[own, :] = y_send[own, :]
 

time: 52.5 us -> 52.4 us (level)
  no operation moved by 1% of the time
where the time goes in v12:
time: 52.4 us; the launch traced here: 52.3 us
  Pallas kernels  51.6 us (98%)
  local copies, waits for them, and re-layouts  0.71 us (1%)
    pallas_call x1, Pallas kernels, on_device(): pl.pallas_call(kernel_body, out_shape=pltpu.VMEM((256, 512), BF16), in_sp...  51.6 us

profile of v12, /device:TPU:1, one launch (start us, length us, event | category | flops | bytes accessed | tf_op | source)
XLA Modules:
  0.0 52.3 jit_solution(15675619532126642194)
XLA Ops:
  0.0 51.6 %hyena.1 = bf16[256,512]{1,0:T(8,128)(2,1)S(1)} custom-call(bf16[256,512]{1,0:T(8,128)(2,1)} %sig_hbm.1, bf16[256,512]{1,0:T(8,128)(2,1)} %gate_hbm.1, f32[256,512]{1,0:T(8,128)} %ker_hbm.1, f32[512]{0:T(512)} %byp_hbm.1, bf16[512,768]{1,0:T(8,128)(2,1)} %constant.10.clone.first_hbm, f32[256,512]{1,0:T(8,128)} %constant.11.clone.turn_hbm, ...), custom_call_target="tpu_custom_call" | custom-call | tf_op jit(solution)/shard_map/hyena/pallas_call | solution.py:358
  51.6 0.7 %copy.11 = bf16[256,512]{1,0:T(8,128)(2,1)} copy(bf16[256,512]{1,0:T(8,128)(2,1)S(1)} %hyena.1) | data formatting | bytes 524288
